TPU v7x, 256 devices: a whole 4x4x8 slice. The times are simulated.
256 devices in a mesh: gx: 32 (over x, z), gy: 8 (over y, core).
Axes of the slice: x: 4, y: 4, z: 8, core: 2. Of those that a mesh axis runs over, the one named last changes fastest.
Arguments:
- right_side: float32 [128, 32, 64, 256], P('gx', 'gy'), may hold values from -6 to 6
- diffusivity: float32 [128, 32, 256], P('gx', 'gy'), may hold values from 1 to 4
- agglomerate: int32 [128, 32, 256], P('gx', 'gy'), may hold values from 0 to 31, as said below
- element_matrix: float32 [64, 64], replicated, may hold values from -0.3 to 4.3, as said below
- face_matrices: float32 [6, 64, 64], replicated, may hold values from -0.375 to 0.375
- restriction: float32 [64], replicated, may hold values from 0.008 to 0.024
- prolongation: float32 [64], replicated, may hold values from 0.5 to 1.5
- coarse_shift: float32 [32, 8, 32], P('gx', 'gy'), may hold values from 0.05 to 0.5
Outputs:
- solution: float32 [128, 32, 64, 256], P('gx', 'gy')
- coarse_correction: float32 [32, 8, 32], P('gx', 'gy')
Inputs may be any that keep to these rules, and one draw needn't show every extreme that they name: `agglomerate`: in every column of 256 elements the values never fall along z and each value from 0 to 31 occurs. `element_matrix`: entries lie within 3.7 to 4.3 on the diagonal and within -0.3 to 0.3 off it.
All inputs are finite; a program needn't handle non-finite values.
Results may differ from a plain program's by a relative error of at most 0.0003.
Values sent between devices are 32-bit elements; how exact they have to be, the bound alone decides.
A program may use at most 64 MiB of HBM per device.

v0:
```python
import jax
import jax.numpy as jnp
from jax import lax
from jax.sharding import PartitionSpec as P

KC = 32
ITC = 24


damping = 0.8
highest = lax.Precision.HIGHEST


def extended(cells, sides, width):
    for axis, dim in sides:
        count = lax.axis_size(axis)
        ends = count - 1
        head = lax.slice_in_dim(cells, 0, width, axis=dim)
        tail = lax.slice_in_dim(cells, cells.shape[dim] - width, cells.shape[dim], axis=dim)
        cells = jnp.concatenate(
            [
                lax.ppermute(tail, axis, [(i, (i + 1) % count) for i in range(ends)]),
                cells,
                lax.ppermute(head, axis, [((i + 1) % count, i) for i in range(ends)]),
            ],
            axis=dim,
        )
    return cells


def apply_local(padded, element_matrix, face_matrices):
    middle = padded[1:-1, 1:-1]
    lined = jnp.pad(middle, ((0, 0), (0, 0), (0, 0), (1, 1)))
    stacked = jnp.stack(
        [
            padded[:-2, 1:-1],
            padded[2:, 1:-1],
            padded[1:-1, :-2],
            padded[1:-1, 2:],
            lined[..., :-2],
            lined[..., 2:],
        ]
    )
    own_term = jnp.einsum("ij,xyjz->xyiz", element_matrix, middle, precision=highest)
    coupled = jnp.einsum("dij,dxyjz->xyiz", face_matrices, stacked, precision=highest)
    return own_term - coupled


def with_faces(values):
    return extended(values, (("gx", 0), ("gy", 1)), 1)


def coarse_step(padded, coarse_rhs, pivots):
    middle = padded[1:-1, 1:-1]
    lined = jnp.pad(middle, ((0, 0), (0, 0), (1, 1)))
    beside_all = padded[:-2, 1:-1] + padded[2:, 1:-1] + padded[1:-1, :-2]
    beside_all = beside_all + padded[1:-1, 2:] + lined[..., :-2] + lined[..., 2:]
    return (coarse_rhs + beside_all) / pivots


def body(
    right_side,
    diffusivity,
    agglomerate,
    element_matrix,
    face_matrices,
    restriction,
    prolongation,
    coarse_shift,
):
    diagonal = jnp.diagonal(element_matrix)[None, None, :, None]
    weight = diffusivity[:, :, None, :]
    source = right_side / weight
    solution = damping * source / diagonal
    solution = (
        solution
        + damping
        * (source - apply_local(with_faces(solution), element_matrix, face_matrices))
        / diagonal
    )
    residual = right_side - weight * apply_local(
        with_faces(solution), element_matrix, face_matrices
    )
    reduced = jnp.einsum("i,xyiz->xyz", restriction, residual, precision=highest)
    levels = jnp.arange(KC, dtype=jnp.int32)
    onehot = (agglomerate[None] == levels[:, None, None, None]).astype(jnp.float32)
    coarse_rhs = jnp.einsum("xyz,kxyz->k", reduced, onehot, precision=highest)[None, None, :]
    pivots = 6.0 + coarse_shift
    current = coarse_rhs / pivots

    def sweep_spread(repeat, values):
        return coarse_step(extended(values, (("gx", 0), ("gy", 1)), 1), coarse_rhs, pivots)

    own_correction = lax.fori_loop(0, ITC - 1, sweep_spread, current)
    lifted = jnp.einsum("k,kxyz->xyz", own_correction[0, 0], onehot, precision=highest)
    solution = solution + prolongation[None, None, :, None] * lifted[:, :, None, :]
    solution = (
        solution
        + damping
        * (source - apply_local(with_faces(solution), element_matrix, face_matrices))
        / diagonal
    )
    return (solution, own_correction)


def solution(mesh):
    return jax.shard_map(
        body,
        mesh=mesh,
        in_specs=(
            P("gx", "gy", None, None),
            P("gx", "gy", None),
            P("gx", "gy", None),
            P(),
            P(),
            P(),
            P(),
            P("gx", "gy", None),
        ),
        out_specs=(P("gx", "gy", None, None), P("gx", "gy", None)),
        check_vma=False,
    )
```

profile of v0, /device:TPU:1, one launch (start us, length us, event | category | flops | bytes accessed | tf_op | source)
XLA Modules:
  0.0 478.9 jit_solution(11115364843907869423)
XLA Ops:
  3.8 4.4 collective-permute-start.4
  17.4 4.8 collective-permute-start.6
  26.9 4.3 collective-permute-done.7
  44.6 5.2 %collective-permute-done.9 = f32[1,4,64,256]{3,2,1,0:T(8,128)S(1)} collective-permute-done((f32[1,4,64,256]{3,2,1,0:T(8,128)S(1)}, f32[1,4,64,256]{3,2,1,0:T(8,128)S(1)}, u32[]{:S(2)}, u32[]{:S(2)}) %collective-permute-start.9) | collective-permute-done | bytes 262176 | tf_op jit(solution)/shard_map/ppermute | solution.py:24
  49.9 4.8 %collective-permute-start.10 = (f32[6,1,64,256]{3,2,1,0:T(8,128)S(1)}, f32[6,1,64,256]{3,2,1,0:T(8,128)S(1)}, u32[]{:S(2)}, u32[]{:S(2)}) collective-permute-start(f32[6,1,64,256]{3,2,1,0:T(8,128)S(1)} %get-tuple-element.67), channel_id=1, source_target_pairs={{0,1},{1,2},{2,3},{3,4},{4,5},{5,6},{6,7},{8,9},{9,10},{10,11},{11... | collective-permute-start | bytes 1179656 | tf_op jit(solution)/shard_map/ppermute | solution.py:22
  59.5 4.4 collective-permute-done.11
  71.1 372.8 %while.12 = (s32[]{:T(128)}, f32[1,1,32]{2,1,0:T(1,128)S(1)}, f32[1,1,32]{2,1,0:T(1,128)S(1)}, f32[1,1,32]{2,1,0:T(1,128)S(1)}, s32[]{:T(128)}) while((s32[]{:T(128)}, f32[1,1,32]{2,1,0:T(1,128)S(1)}, f32[1,1,32]{2,1,0:T(1,128)S(1)}, f32[1,1,32]{2,1,0:T(1,128)S(1)}, s32[]{:T(128)}) %tuple.38), condition=%wide.region_1.2_spmd, body=%wide.region_0.1_spmd.sunk | while | flops 226 | bytes 8285 | solution.py:94
  71.1 4.6 collective-permute-start
  96.8 5.3 %collective-permute-start.3 = (f32[3,1,32]{2,1,0:T(1,128)S(1)}, f32[3,1,32]{2,1,0:T(1,128)S(1)}, u32[]{:S(2)}, u32[]{:S(2)}) collective-permute-start(f32[3,1,32]{2,1,0:T(1,128)S(1)} %constant_dynamic-update-slice_fusion.8), channel_id=1, source_target_pairs={{0,1},{1,2},{2,3},{3,4},{4,5},{5,6},{6,7},{8,9},{9,10},{10,11},{11... | collective-permute-start | bytes 1160 | tf_op jit(solution)/shard_map/while/body/eval_jaxpr/ppermute | solution.py:22
  111.7 5.6 %collective-permute-start.3 = (f32[3,1,32]{2,1,0:T(1,128)S(1)}, f32[3,1,32]{2,1,0:T(1,128)S(1)}, u32[]{:S(2)}, u32[]{:S(2)}) collective-permute-start(f32[3,1,32]{2,1,0:T(1,128)S(1)} %constant_dynamic-update-slice_fusion.8), channel_id=1, source_target_pairs={{0,1},{1,2},{2,3},{3,4},{4,5},{5,6},{6,7},{8,9},{9,10},{10,11},{11... | collective-permute-start | bytes 1160 | tf_op jit(solution)/shard_map/while/body/eval_jaxpr/ppermute | solution.py:22
  127.4 5.6 %collective-permute-start.3 = (f32[3,1,32]{2,1,0:T(1,128)S(1)}, f32[3,1,32]{2,1,0:T(1,128)S(1)}, u32[]{:S(2)}, u32[]{:S(2)}) collective-permute-start(f32[3,1,32]{2,1,0:T(1,128)S(1)} %constant_dynamic-update-slice_fusion.8), channel_id=1, source_target_pairs={{0,1},{1,2},{2,3},{3,4},{4,5},{5,6},{6,7},{8,9},{9,10},{10,11},{11... | collective-permute-start | bytes 1160 | tf_op jit(solution)/shard_map/while/body/eval_jaxpr/ppermute | solution.py:22
  143.1 5.5 %collective-permute-start.3 = (f32[3,1,32]{2,1,0:T(1,128)S(1)}, f32[3,1,32]{2,1,0:T(1,128)S(1)}, u32[]{:S(2)}, u32[]{:S(2)}) collective-permute-start(f32[3,1,32]{2,1,0:T(1,128)S(1)} %constant_dynamic-update-slice_fusion.8), channel_id=1, source_target_pairs={{0,1},{1,2},{2,3},{3,4},{4,5},{5,6},{6,7},{8,9},{9,10},{10,11},{11... | collective-permute-start | bytes 1160 | tf_op jit(solution)/shard_map/while/body/eval_jaxpr/ppermute | solution.py:22
  159.4 5.3 %collective-permute-start.3 = (f32[3,1,32]{2,1,0:T(1,128)S(1)}, f32[3,1,32]{2,1,0:T(1,128)S(1)}, u32[]{:S(2)}, u32[]{:S(2)}) collective-permute-start(f32[3,1,32]{2,1,0:T(1,128)S(1)} %constant_dynamic-update-slice_fusion.8), channel_id=1, source_target_pairs={{0,1},{1,2},{2,3},{3,4},{4,5},{5,6},{6,7},{8,9},{9,10},{10,11},{11... | collective-permute-start | bytes 1160 | tf_op jit(solution)/shard_map/while/body/eval_jaxpr/ppermute | solution.py:22
  175.9 5.3 %collective-permute-start.3 = (f32[3,1,32]{2,1,0:T(1,128)S(1)}, f32[3,1,32]{2,1,0:T(1,128)S(1)}, u32[]{:S(2)}, u32[]{:S(2)}) collective-permute-start(f32[3,1,32]{2,1,0:T(1,128)S(1)} %constant_dynamic-update-slice_fusion.8), channel_id=1, source_target_pairs={{0,1},{1,2},{2,3},{3,4},{4,5},{5,6},{6,7},{8,9},{9,10},{10,11},{11... | collective-permute-start | bytes 1160 | tf_op jit(solution)/shard_map/while/body/eval_jaxpr/ppermute | solution.py:22
  192.2 5.3 %collective-permute-start.3 = (f32[3,1,32]{2,1,0:T(1,128)S(1)}, f32[3,1,32]{2,1,0:T(1,128)S(1)}, u32[]{:S(2)}, u32[]{:S(2)}) collective-permute-start(f32[3,1,32]{2,1,0:T(1,128)S(1)} %constant_dynamic-update-slice_fusion.8), channel_id=1, source_target_pairs={{0,1},{1,2},{2,3},{3,4},{4,5},{5,6},{6,7},{8,9},{9,10},{10,11},{11... | collective-permute-start | bytes 1160 | tf_op jit(solution)/shard_map/while/body/eval_jaxpr/ppermute | solution.py:22
  208.6 5.3 %collective-permute-start.3 = (f32[3,1,32]{2,1,0:T(1,128)S(1)}, f32[3,1,32]{2,1,0:T(1,128)S(1)}, u32[]{:S(2)}, u32[]{:S(2)}) collective-permute-start(f32[3,1,32]{2,1,0:T(1,128)S(1)} %constant_dynamic-update-slice_fusion.8), channel_id=1, source_target_pairs={{0,1},{1,2},{2,3},{3,4},{4,5},{5,6},{6,7},{8,9},{9,10},{10,11},{11... | collective-permute-start | bytes 1160 | tf_op jit(solution)/shard_map/while/body/eval_jaxpr/ppermute | solution.py:22
  225.0 5.3 %collective-permute-start.3 = (f32[3,1,32]{2,1,0:T(1,128)S(1)}, f32[3,1,32]{2,1,0:T(1,128)S(1)}, u32[]{:S(2)}, u32[]{:S(2)}) collective-permute-start(f32[3,1,32]{2,1,0:T(1,128)S(1)} %constant_dynamic-update-slice_fusion.8), channel_id=1, source_target_pairs={{0,1},{1,2},{2,3},{3,4},{4,5},{5,6},{6,7},{8,9},{9,10},{10,11},{11... | collective-permute-start | bytes 1160 | tf_op jit(solution)/shard_map/while/body/eval_jaxpr/ppermute | solution.py:22
  241.3 5.3 %collective-permute-start.3 = (f32[3,1,32]{2,1,0:T(1,128)S(1)}, f32[3,1,32]{2,1,0:T(1,128)S(1)}, u32[]{:S(2)}, u32[]{:S(2)}) collective-permute-start(f32[3,1,32]{2,1,0:T(1,128)S(1)} %constant_dynamic-update-slice_fusion.8), channel_id=1, source_target_pairs={{0,1},{1,2},{2,3},{3,4},{4,5},{5,6},{6,7},{8,9},{9,10},{10,11},{11... | collective-permute-start | bytes 1160 | tf_op jit(solution)/shard_map/while/body/eval_jaxpr/ppermute | solution.py:22
  257.7 5.3 %collective-permute-start.3 = (f32[3,1,32]{2,1,0:T(1,128)S(1)}, f32[3,1,32]{2,1,0:T(1,128)S(1)}, u32[]{:S(2)}, u32[]{:S(2)}) collective-permute-start(f32[3,1,32]{2,1,0:T(1,128)S(1)} %constant_dynamic-update-slice_fusion.8), channel_id=1, source_target_pairs={{0,1},{1,2},{2,3},{3,4},{4,5},{5,6},{6,7},{8,9},{9,10},{10,11},{11... | collective-permute-start | bytes 1160 | tf_op jit(solution)/shard_map/while/body/eval_jaxpr/ppermute | solution.py:22
  274.1 5.3 %collective-permute-start.3 = (f32[3,1,32]{2,1,0:T(1,128)S(1)}, f32[3,1,32]{2,1,0:T(1,128)S(1)}, u32[]{:S(2)}, u32[]{:S(2)}) collective-permute-start(f32[3,1,32]{2,1,0:T(1,128)S(1)} %constant_dynamic-update-slice_fusion.8), channel_id=1, source_target_pairs={{0,1},{1,2},{2,3},{3,4},{4,5},{5,6},{6,7},{8,9},{9,10},{10,11},{11... | collective-permute-start | bytes 1160 | tf_op jit(solution)/shard_map/while/body/eval_jaxpr/ppermute | solution.py:22
  290.5 5.3 %collective-permute-start.3 = (f32[3,1,32]{2,1,0:T(1,128)S(1)}, f32[3,1,32]{2,1,0:T(1,128)S(1)}, u32[]{:S(2)}, u32[]{:S(2)}) collective-permute-start(f32[3,1,32]{2,1,0:T(1,128)S(1)} %constant_dynamic-update-slice_fusion.8), channel_id=1, source_target_pairs={{0,1},{1,2},{2,3},{3,4},{4,5},{5,6},{6,7},{8,9},{9,10},{10,11},{11... | collective-permute-start | bytes 1160 | tf_op jit(solution)/shard_map/while/body/eval_jaxpr/ppermute | solution.py:22
  306.8 5.3 %collective-permute-start.3 = (f32[3,1,32]{2,1,0:T(1,128)S(1)}, f32[3,1,32]{2,1,0:T(1,128)S(1)}, u32[]{:S(2)}, u32[]{:S(2)}) collective-permute-start(f32[3,1,32]{2,1,0:T(1,128)S(1)} %constant_dynamic-update-slice_fusion.8), channel_id=1, source_target_pairs={{0,1},{1,2},{2,3},{3,4},{4,5},{5,6},{6,7},{8,9},{9,10},{10,11},{11... | collective-permute-start | bytes 1160 | tf_op jit(solution)/shard_map/while/body/eval_jaxpr/ppermute | solution.py:22
  323.2 5.3 %collective-permute-start.3 = (f32[3,1,32]{2,1,0:T(1,128)S(1)}, f32[3,1,32]{2,1,0:T(1,128)S(1)}, u32[]{:S(2)}, u32[]{:S(2)}) collective-permute-start(f32[3,1,32]{2,1,0:T(1,128)S(1)} %constant_dynamic-update-slice_fusion.8), channel_id=1, source_target_pairs={{0,1},{1,2},{2,3},{3,4},{4,5},{5,6},{6,7},{8,9},{9,10},{10,11},{11... | collective-permute-start | bytes 1160 | tf_op jit(solution)/shard_map/while/body/eval_jaxpr/ppermute | solution.py:22
  339.6 5.3 %collective-permute-start.3 = (f32[3,1,32]{2,1,0:T(1,128)S(1)}, f32[3,1,32]{2,1,0:T(1,128)S(1)}, u32[]{:S(2)}, u32[]{:S(2)}) collective-permute-start(f32[3,1,32]{2,1,0:T(1,128)S(1)} %constant_dynamic-update-slice_fusion.8), channel_id=1, source_target_pairs={{0,1},{1,2},{2,3},{3,4},{4,5},{5,6},{6,7},{8,9},{9,10},{10,11},{11... | collective-permute-start | bytes 1160 | tf_op jit(solution)/shard_map/while/body/eval_jaxpr/ppermute | solution.py:22
  355.9 5.3 %collective-permute-start.3 = (f32[3,1,32]{2,1,0:T(1,128)S(1)}, f32[3,1,32]{2,1,0:T(1,128)S(1)}, u32[]{:S(2)}, u32[]{:S(2)}) collective-permute-start(f32[3,1,32]{2,1,0:T(1,128)S(1)} %constant_dynamic-update-slice_fusion.8), channel_id=1, source_target_pairs={{0,1},{1,2},{2,3},{3,4},{4,5},{5,6},{6,7},{8,9},{9,10},{10,11},{11... | collective-permute-start | bytes 1160 | tf_op jit(solution)/shard_map/while/body/eval_jaxpr/ppermute | solution.py:22
  372.3 5.3 %collective-permute-start.3 = (f32[3,1,32]{2,1,0:T(1,128)S(1)}, f32[3,1,32]{2,1,0:T(1,128)S(1)}, u32[]{:S(2)}, u32[]{:S(2)}) collective-permute-start(f32[3,1,32]{2,1,0:T(1,128)S(1)} %constant_dynamic-update-slice_fusion.8), channel_id=1, source_target_pairs={{0,1},{1,2},{2,3},{3,4},{4,5},{5,6},{6,7},{8,9},{9,10},{10,11},{11... | collective-permute-start | bytes 1160 | tf_op jit(solution)/shard_map/while/body/eval_jaxpr/ppermute | solution.py:22
  388.7 5.3 %collective-permute-start.3 = (f32[3,1,32]{2,1,0:T(1,128)S(1)}, f32[3,1,32]{2,1,0:T(1,128)S(1)}, u32[]{:S(2)}, u32[]{:S(2)}) collective-permute-start(f32[3,1,32]{2,1,0:T(1,128)S(1)} %constant_dynamic-update-slice_fusion.8), channel_id=1, source_target_pairs={{0,1},{1,2},{2,3},{3,4},{4,5},{5,6},{6,7},{8,9},{9,10},{10,11},{11... | collective-permute-start | bytes 1160 | tf_op jit(solution)/shard_map/while/body/eval_jaxpr/ppermute | solution.py:22
  405.0 5.3 %collective-permute-start.3 = (f32[3,1,32]{2,1,0:T(1,128)S(1)}, f32[3,1,32]{2,1,0:T(1,128)S(1)}, u32[]{:S(2)}, u32[]{:S(2)}) collective-permute-start(f32[3,1,32]{2,1,0:T(1,128)S(1)} %constant_dynamic-update-slice_fusion.8), channel_id=1, source_target_pairs={{0,1},{1,2},{2,3},{3,4},{4,5},{5,6},{6,7},{8,9},{9,10},{10,11},{11... | collective-permute-start | bytes 1160 | tf_op jit(solution)/shard_map/while/body/eval_jaxpr/ppermute | solution.py:22
  421.4 5.3 %collective-permute-start.3 = (f32[3,1,32]{2,1,0:T(1,128)S(1)}, f32[3,1,32]{2,1,0:T(1,128)S(1)}, u32[]{:S(2)}, u32[]{:S(2)}) collective-permute-start(f32[3,1,32]{2,1,0:T(1,128)S(1)} %constant_dynamic-update-slice_fusion.8), channel_id=1, source_target_pairs={{0,1},{1,2},{2,3},{3,4},{4,5},{5,6},{6,7},{8,9},{9,10},{10,11},{11... | collective-permute-start | bytes 1160 | tf_op jit(solution)/shard_map/while/body/eval_jaxpr/ppermute | solution.py:22
  437.8 5.3 %collective-permute-start.3 = (f32[3,1,32]{2,1,0:T(1,128)S(1)}, f32[3,1,32]{2,1,0:T(1,128)S(1)}, u32[]{:S(2)}, u32[]{:S(2)}) collective-permute-start(f32[3,1,32]{2,1,0:T(1,128)S(1)} %constant_dynamic-update-slice_fusion.8), channel_id=1, source_target_pairs={{0,1},{1,2},{2,3},{3,4},{4,5},{5,6},{6,7},{8,9},{9,10},{10,11},{11... | collective-permute-start | bytes 1160 | tf_op jit(solution)/shard_map/while/body/eval_jaxpr/ppermute | solution.py:22
  456.1 6.5 %collective-permute-start.14 = (f32[6,1,64,256]{3,2,1,0:T(8,128)S(1)}, f32[6,1,64,256]{3,2,1,0:T(8,128)S(1)}, u32[]{:S(2)}, u32[]{:S(2)}) collective-permute-start(f32[6,1,64,256]{3,2,1,0:T(8,128)S(1)} %get-tuple-element.65), channel_id=1, source_target_pairs={{0,1},{1,2},{2,3},{3,4},{4,5},{5,6},{6,7},{8,9},{9,10},{10,11},{11... | collective-permute-start | bytes 1179656 | tf_op jit(solution)/shard_map/ppermute | solution.py:22
  467.4 4.3 collective-permute-done.15
  (350 shorter events, 315.1 us)
Async XLA Ops:
  3.8 9.3 %collective-permute-start.4 = (f32[1,4,64,256]{3,2,1,0:T(8,128)S(1)}, f32[1,4,64,256]{3,2,1,0:T(8,128)S(1)}, u32[]{:S(2)}, u32[]{:S(2)}) collective-permute-start(f32[1,4,64,256]{3,2,1,0:T(8,128)S(1)} %get-tuple-element.75), channel_id=1, source_target_pairs={{0,8},{8,16},{16,24},{24,32},{32,40},{40,48},{48,56},{56,64},{64,7... | collective-permute-start | bytes 786440 | tf_op jit(solution)/shard_map/ppermute | solution.py:22
  8.2 9.1 %collective-permute-start.5 = (f32[1,4,64,256]{3,2,1,0:T(8,128)S(1)}, f32[1,4,64,256]{3,2,1,0:T(8,128)S(1)}, u32[]{:S(2)}, u32[]{:S(2)}) collective-permute-start(f32[1,4,64,256]{3,2,1,0:T(8,128)S(1)} %get-tuple-element.74), channel_id=1, source_target_pairs={{8,0},{16,8},{24,16},{32,24},{40,32},{48,40},{56,48},{64,56},{72,6... | collective-permute-start | bytes 786440 | tf_op jit(solution)/shard_map/ppermute | solution.py:24
  17.4 9.5 %collective-permute-start.6 = (f32[6,1,64,256]{3,2,1,0:T(8,128)S(1)}, f32[6,1,64,256]{3,2,1,0:T(8,128)S(1)}, u32[]{:S(2)}, u32[]{:S(2)}) collective-permute-start(f32[6,1,64,256]{3,2,1,0:T(8,128)S(1)} %get-tuple-element.69), channel_id=1, source_target_pairs={{0,1},{1,2},{2,3},{3,4},{4,5},{5,6},{6,7},{8,9},{9,10},{10,11},{11... | collective-permute-start | bytes 1179656 | tf_op jit(solution)/shard_map/ppermute | solution.py:22
  22.1 9.1 %collective-permute-start.7 = (f32[6,1,64,256]{3,2,1,0:T(8,128)S(1)}, f32[6,1,64,256]{3,2,1,0:T(8,128)S(1)}, u32[]{:S(2)}, u32[]{:S(2)}) collective-permute-start(f32[6,1,64,256]{3,2,1,0:T(8,128)S(1)} %get-tuple-element.68), channel_id=1, source_target_pairs={{1,0},{2,1},{3,2},{4,3},{5,4},{6,5},{7,6},{9,8},{10,9},{11,10},{12... | collective-permute-start | bytes 1179656 | tf_op jit(solution)/shard_map/ppermute | solution.py:24
  41.3 8.5 %collective-permute-start.9 = (f32[1,4,64,256]{3,2,1,0:T(8,128)S(1)}, f32[1,4,64,256]{3,2,1,0:T(8,128)S(1)}, u32[]{:S(2)}, u32[]{:S(2)}) collective-permute-start(f32[1,4,64,256]{3,2,1,0:T(8,128)S(1)} %get-tuple-element.72), channel_id=1, source_target_pairs={{8,0},{16,8},{24,16},{32,24},{40,32},{48,40},{56,48},{64,56},{72,6... | collective-permute-start | bytes 786440 | tf_op jit(solution)/shard_map/ppermute | solution.py:24
  49.9 9.5 %collective-permute-start.10 = (f32[6,1,64,256]{3,2,1,0:T(8,128)S(1)}, f32[6,1,64,256]{3,2,1,0:T(8,128)S(1)}, u32[]{:S(2)}, u32[]{:S(2)}) collective-permute-start(f32[6,1,64,256]{3,2,1,0:T(8,128)S(1)} %get-tuple-element.67), channel_id=1, source_target_pairs={{0,1},{1,2},{2,3},{3,4},{4,5},{5,6},{6,7},{8,9},{9,10},{10,11},{11... | collective-permute-start | bytes 1179656 | tf_op jit(solution)/shard_map/ppermute | solution.py:22
  54.9 9.1 %collective-permute-start.11 = (f32[6,1,64,256]{3,2,1,0:T(8,128)S(1)}, f32[6,1,64,256]{3,2,1,0:T(8,128)S(1)}, u32[]{:S(2)}, u32[]{:S(2)}) collective-permute-start(f32[6,1,64,256]{3,2,1,0:T(8,128)S(1)} %get-tuple-element.66), channel_id=1, source_target_pairs={{1,0},{2,1},{3,2},{4,3},{5,4},{6,5},{7,6},{9,8},{10,9},{11,10},{12... | collective-permute-start | bytes 1179656 | tf_op jit(solution)/shard_map/ppermute | solution.py:24
  94.6 7.5 %collective-permute-start.2 = (f32[3,1,32]{2,1,0:T(1,128)S(1)}, f32[3,1,32]{2,1,0:T(1,128)S(1)}, u32[]{:S(2)}, u32[]{:S(2)}) collective-permute-start(f32[3,1,32]{2,1,0:T(1,128)S(1)} %constant_dynamic-update-slice_fusion.8), channel_id=1, source_target_pairs={{1,0},{2,1},{3,2},{4,3},{5,4},{6,5},{7,6},{9,8},{10,9},{11,10},{12... | collective-permute-start | bytes 1160 | tf_op jit(solution)/shard_map/while/body/eval_jaxpr/ppermute | solution.py:24
  109.8 7.5 %collective-permute-start.2 = (f32[3,1,32]{2,1,0:T(1,128)S(1)}, f32[3,1,32]{2,1,0:T(1,128)S(1)}, u32[]{:S(2)}, u32[]{:S(2)}) collective-permute-start(f32[3,1,32]{2,1,0:T(1,128)S(1)} %constant_dynamic-update-slice_fusion.8), channel_id=1, source_target_pairs={{1,0},{2,1},{3,2},{4,3},{5,4},{6,5},{7,6},{9,8},{10,9},{11,10},{12... | collective-permute-start | bytes 1160 | tf_op jit(solution)/shard_map/while/body/eval_jaxpr/ppermute | solution.py:24
  125.5 7.5 %collective-permute-start.2 = (f32[3,1,32]{2,1,0:T(1,128)S(1)}, f32[3,1,32]{2,1,0:T(1,128)S(1)}, u32[]{:S(2)}, u32[]{:S(2)}) collective-permute-start(f32[3,1,32]{2,1,0:T(1,128)S(1)} %constant_dynamic-update-slice_fusion.8), channel_id=1, source_target_pairs={{1,0},{2,1},{3,2},{4,3},{5,4},{6,5},{7,6},{9,8},{10,9},{11,10},{12... | collective-permute-start | bytes 1160 | tf_op jit(solution)/shard_map/while/body/eval_jaxpr/ppermute | solution.py:24
  141.2 7.5 %collective-permute-start.2 = (f32[3,1,32]{2,1,0:T(1,128)S(1)}, f32[3,1,32]{2,1,0:T(1,128)S(1)}, u32[]{:S(2)}, u32[]{:S(2)}) collective-permute-start(f32[3,1,32]{2,1,0:T(1,128)S(1)} %constant_dynamic-update-slice_fusion.8), channel_id=1, source_target_pairs={{1,0},{2,1},{3,2},{4,3},{5,4},{6,5},{7,6},{9,8},{10,9},{11,10},{12... | collective-permute-start | bytes 1160 | tf_op jit(solution)/shard_map/while/body/eval_jaxpr/ppermute | solution.py:24
  157.5 7.3 %collective-permute-start.2 = (f32[3,1,32]{2,1,0:T(1,128)S(1)}, f32[3,1,32]{2,1,0:T(1,128)S(1)}, u32[]{:S(2)}, u32[]{:S(2)}) collective-permute-start(f32[3,1,32]{2,1,0:T(1,128)S(1)} %constant_dynamic-update-slice_fusion.8), channel_id=1, source_target_pairs={{1,0},{2,1},{3,2},{4,3},{5,4},{6,5},{7,6},{9,8},{10,9},{11,10},{12... | collective-permute-start | bytes 1160 | tf_op jit(solution)/shard_map/while/body/eval_jaxpr/ppermute | solution.py:24
  174.0 7.3 %collective-permute-start.2 = (f32[3,1,32]{2,1,0:T(1,128)S(1)}, f32[3,1,32]{2,1,0:T(1,128)S(1)}, u32[]{:S(2)}, u32[]{:S(2)}) collective-permute-start(f32[3,1,32]{2,1,0:T(1,128)S(1)} %constant_dynamic-update-slice_fusion.8), channel_id=1, source_target_pairs={{1,0},{2,1},{3,2},{4,3},{5,4},{6,5},{7,6},{9,8},{10,9},{11,10},{12... | collective-permute-start | bytes 1160 | tf_op jit(solution)/shard_map/while/body/eval_jaxpr/ppermute | solution.py:24
  190.3 7.3 %collective-permute-start.2 = (f32[3,1,32]{2,1,0:T(1,128)S(1)}, f32[3,1,32]{2,1,0:T(1,128)S(1)}, u32[]{:S(2)}, u32[]{:S(2)}) collective-permute-start(f32[3,1,32]{2,1,0:T(1,128)S(1)} %constant_dynamic-update-slice_fusion.8), channel_id=1, source_target_pairs={{1,0},{2,1},{3,2},{4,3},{5,4},{6,5},{7,6},{9,8},{10,9},{11,10},{12... | collective-permute-start | bytes 1160 | tf_op jit(solution)/shard_map/while/body/eval_jaxpr/ppermute | solution.py:24
  206.7 7.3 %collective-permute-start.2 = (f32[3,1,32]{2,1,0:T(1,128)S(1)}, f32[3,1,32]{2,1,0:T(1,128)S(1)}, u32[]{:S(2)}, u32[]{:S(2)}) collective-permute-start(f32[3,1,32]{2,1,0:T(1,128)S(1)} %constant_dynamic-update-slice_fusion.8), channel_id=1, source_target_pairs={{1,0},{2,1},{3,2},{4,3},{5,4},{6,5},{7,6},{9,8},{10,9},{11,10},{12... | collective-permute-start | bytes 1160 | tf_op jit(solution)/shard_map/while/body/eval_jaxpr/ppermute | solution.py:24
  223.1 7.3 %collective-permute-start.2 = (f32[3,1,32]{2,1,0:T(1,128)S(1)}, f32[3,1,32]{2,1,0:T(1,128)S(1)}, u32[]{:S(2)}, u32[]{:S(2)}) collective-permute-start(f32[3,1,32]{2,1,0:T(1,128)S(1)} %constant_dynamic-update-slice_fusion.8), channel_id=1, source_target_pairs={{1,0},{2,1},{3,2},{4,3},{5,4},{6,5},{7,6},{9,8},{10,9},{11,10},{12... | collective-permute-start | bytes 1160 | tf_op jit(solution)/shard_map/while/body/eval_jaxpr/ppermute | solution.py:24
  239.4 7.3 %collective-permute-start.2 = (f32[3,1,32]{2,1,0:T(1,128)S(1)}, f32[3,1,32]{2,1,0:T(1,128)S(1)}, u32[]{:S(2)}, u32[]{:S(2)}) collective-permute-start(f32[3,1,32]{2,1,0:T(1,128)S(1)} %constant_dynamic-update-slice_fusion.8), channel_id=1, source_target_pairs={{1,0},{2,1},{3,2},{4,3},{5,4},{6,5},{7,6},{9,8},{10,9},{11,10},{12... | collective-permute-start | bytes 1160 | tf_op jit(solution)/shard_map/while/body/eval_jaxpr/ppermute | solution.py:24
  255.8 7.3 %collective-permute-start.2 = (f32[3,1,32]{2,1,0:T(1,128)S(1)}, f32[3,1,32]{2,1,0:T(1,128)S(1)}, u32[]{:S(2)}, u32[]{:S(2)}) collective-permute-start(f32[3,1,32]{2,1,0:T(1,128)S(1)} %constant_dynamic-update-slice_fusion.8), channel_id=1, source_target_pairs={{1,0},{2,1},{3,2},{4,3},{5,4},{6,5},{7,6},{9,8},{10,9},{11,10},{12... | collective-permute-start | bytes 1160 | tf_op jit(solution)/shard_map/while/body/eval_jaxpr/ppermute | solution.py:24
  272.2 7.3 %collective-permute-start.2 = (f32[3,1,32]{2,1,0:T(1,128)S(1)}, f32[3,1,32]{2,1,0:T(1,128)S(1)}, u32[]{:S(2)}, u32[]{:S(2)}) collective-permute-start(f32[3,1,32]{2,1,0:T(1,128)S(1)} %constant_dynamic-update-slice_fusion.8), channel_id=1, source_target_pairs={{1,0},{2,1},{3,2},{4,3},{5,4},{6,5},{7,6},{9,8},{10,9},{11,10},{12... | collective-permute-start | bytes 1160 | tf_op jit(solution)/shard_map/while/body/eval_jaxpr/ppermute | solution.py:24
  288.5 7.3 %collective-permute-start.2 = (f32[3,1,32]{2,1,0:T(1,128)S(1)}, f32[3,1,32]{2,1,0:T(1,128)S(1)}, u32[]{:S(2)}, u32[]{:S(2)}) collective-permute-start(f32[3,1,32]{2,1,0:T(1,128)S(1)} %constant_dynamic-update-slice_fusion.8), channel_id=1, source_target_pairs={{1,0},{2,1},{3,2},{4,3},{5,4},{6,5},{7,6},{9,8},{10,9},{11,10},{12... | collective-permute-start | bytes 1160 | tf_op jit(solution)/shard_map/while/body/eval_jaxpr/ppermute | solution.py:24
  304.9 7.3 %collective-permute-start.2 = (f32[3,1,32]{2,1,0:T(1,128)S(1)}, f32[3,1,32]{2,1,0:T(1,128)S(1)}, u32[]{:S(2)}, u32[]{:S(2)}) collective-permute-start(f32[3,1,32]{2,1,0:T(1,128)S(1)} %constant_dynamic-update-slice_fusion.8), channel_id=1, source_target_pairs={{1,0},{2,1},{3,2},{4,3},{5,4},{6,5},{7,6},{9,8},{10,9},{11,10},{12... | collective-permute-start | bytes 1160 | tf_op jit(solution)/shard_map/while/body/eval_jaxpr/ppermute | solution.py:24
  321.3 7.3 %collective-permute-start.2 = (f32[3,1,32]{2,1,0:T(1,128)S(1)}, f32[3,1,32]{2,1,0:T(1,128)S(1)}, u32[]{:S(2)}, u32[]{:S(2)}) collective-permute-start(f32[3,1,32]{2,1,0:T(1,128)S(1)} %constant_dynamic-update-slice_fusion.8), channel_id=1, source_target_pairs={{1,0},{2,1},{3,2},{4,3},{5,4},{6,5},{7,6},{9,8},{10,9},{11,10},{12... | collective-permute-start | bytes 1160 | tf_op jit(solution)/shard_map/while/body/eval_jaxpr/ppermute | solution.py:24
  337.6 7.3 %collective-permute-start.2 = (f32[3,1,32]{2,1,0:T(1,128)S(1)}, f32[3,1,32]{2,1,0:T(1,128)S(1)}, u32[]{:S(2)}, u32[]{:S(2)}) collective-permute-start(f32[3,1,32]{2,1,0:T(1,128)S(1)} %constant_dynamic-update-slice_fusion.8), channel_id=1, source_target_pairs={{1,0},{2,1},{3,2},{4,3},{5,4},{6,5},{7,6},{9,8},{10,9},{11,10},{12... | collective-permute-start | bytes 1160 | tf_op jit(solution)/shard_map/while/body/eval_jaxpr/ppermute | solution.py:24
  354.0 7.3 %collective-permute-start.2 = (f32[3,1,32]{2,1,0:T(1,128)S(1)}, f32[3,1,32]{2,1,0:T(1,128)S(1)}, u32[]{:S(2)}, u32[]{:S(2)}) collective-permute-start(f32[3,1,32]{2,1,0:T(1,128)S(1)} %constant_dynamic-update-slice_fusion.8), channel_id=1, source_target_pairs={{1,0},{2,1},{3,2},{4,3},{5,4},{6,5},{7,6},{9,8},{10,9},{11,10},{12... | collective-permute-start | bytes 1160 | tf_op jit(solution)/shard_map/while/body/eval_jaxpr/ppermute | solution.py:24
  370.4 7.3 %collective-permute-start.2 = (f32[3,1,32]{2,1,0:T(1,128)S(1)}, f32[3,1,32]{2,1,0:T(1,128)S(1)}, u32[]{:S(2)}, u32[]{:S(2)}) collective-permute-start(f32[3,1,32]{2,1,0:T(1,128)S(1)} %constant_dynamic-update-slice_fusion.8), channel_id=1, source_target_pairs={{1,0},{2,1},{3,2},{4,3},{5,4},{6,5},{7,6},{9,8},{10,9},{11,10},{12... | collective-permute-start | bytes 1160 | tf_op jit(solution)/shard_map/while/body/eval_jaxpr/ppermute | solution.py:24
  386.8 7.3 %collective-permute-start.2 = (f32[3,1,32]{2,1,0:T(1,128)S(1)}, f32[3,1,32]{2,1,0:T(1,128)S(1)}, u32[]{:S(2)}, u32[]{:S(2)}) collective-permute-start(f32[3,1,32]{2,1,0:T(1,128)S(1)} %constant_dynamic-update-slice_fusion.8), channel_id=1, source_target_pairs={{1,0},{2,1},{3,2},{4,3},{5,4},{6,5},{7,6},{9,8},{10,9},{11,10},{12... | collective-permute-start | bytes 1160 | tf_op jit(solution)/shard_map/while/body/eval_jaxpr/ppermute | solution.py:24
  403.1 7.3 %collective-permute-start.2 = (f32[3,1,32]{2,1,0:T(1,128)S(1)}, f32[3,1,32]{2,1,0:T(1,128)S(1)}, u32[]{:S(2)}, u32[]{:S(2)}) collective-permute-start(f32[3,1,32]{2,1,0:T(1,128)S(1)} %constant_dynamic-update-slice_fusion.8), channel_id=1, source_target_pairs={{1,0},{2,1},{3,2},{4,3},{5,4},{6,5},{7,6},{9,8},{10,9},{11,10},{12... | collective-permute-start | bytes 1160 | tf_op jit(solution)/shard_map/while/body/eval_jaxpr/ppermute | solution.py:24
  419.5 7.3 %collective-permute-start.2 = (f32[3,1,32]{2,1,0:T(1,128)S(1)}, f32[3,1,32]{2,1,0:T(1,128)S(1)}, u32[]{:S(2)}, u32[]{:S(2)}) collective-permute-start(f32[3,1,32]{2,1,0:T(1,128)S(1)} %constant_dynamic-update-slice_fusion.8), channel_id=1, source_target_pairs={{1,0},{2,1},{3,2},{4,3},{5,4},{6,5},{7,6},{9,8},{10,9},{11,10},{12... | collective-permute-start | bytes 1160 | tf_op jit(solution)/shard_map/while/body/eval_jaxpr/ppermute | solution.py:24
  444.5 7.5 %collective-permute-start.12 = (f32[1,4,64,256]{3,2,1,0:T(8,128)S(1)}, f32[1,4,64,256]{3,2,1,0:T(8,128)S(1)}, u32[]{:S(2)}, u32[]{:S(2)}) collective-permute-start(f32[1,4,64,256]{3,2,1,0:T(8,128)S(1)} %get-tuple-element.71), channel_id=1, source_target_pairs={{0,8},{8,16},{16,24},{24,32},{32,40},{40,48},{48,56},{56,64},{64,7... | collective-permute-start | bytes 786440 | tf_op jit(solution)/shard_map/ppermute | solution.py:22
  448.2 7.8 %collective-permute-start.13 = (f32[1,4,64,256]{3,2,1,0:T(8,128)S(1)}, f32[1,4,64,256]{3,2,1,0:T(8,128)S(1)}, u32[]{:S(2)}, u32[]{:S(2)}) collective-permute-start(f32[1,4,64,256]{3,2,1,0:T(8,128)S(1)} %get-tuple-element.70), channel_id=1, source_target_pairs={{8,0},{16,8},{24,16},{32,24},{40,32},{48,40},{56,48},{64,56},{72,6... | collective-permute-start | bytes 786440 | tf_op jit(solution)/shard_map/ppermute | solution.py:24
  456.1 11.2 %collective-permute-start.14 = (f32[6,1,64,256]{3,2,1,0:T(8,128)S(1)}, f32[6,1,64,256]{3,2,1,0:T(8,128)S(1)}, u32[]{:S(2)}, u32[]{:S(2)}) collective-permute-start(f32[6,1,64,256]{3,2,1,0:T(8,128)S(1)} %get-tuple-element.65), channel_id=1, source_target_pairs={{0,1},{1,2},{2,3},{3,4},{4,5},{5,6},{6,7},{8,9},{9,10},{10,11},{11... | collective-permute-start | bytes 1179656 | tf_op jit(solution)/shard_map/ppermute | solution.py:22
  462.6 9.1 %collective-permute-start.15 = (f32[6,1,64,256]{3,2,1,0:T(8,128)S(1)}, f32[6,1,64,256]{3,2,1,0:T(8,128)S(1)}, u32[]{:S(2)}, u32[]{:S(2)}) collective-permute-start(f32[6,1,64,256]{3,2,1,0:T(8,128)S(1)} %get-tuple-element.64), channel_id=1, source_target_pairs={{1,0},{2,1},{3,2},{4,3},{5,4},{6,5},{7,6},{9,8},{10,9},{11,10},{12... | collective-permute-start | bytes 1179656 | tf_op jit(solution)/shard_map/ppermute | solution.py:24
  (81 other events, 854.5 us)
where the time goes:
time: 485 us; the launch traced here: 479 us
  starting transfers between devices  317 us (65%)
  waiting for transfers between devices  132 us (27%)
  matrix products  18.5 us (4%)
  other arithmetic  4.88 us (1%)
    ppermute x52, starting transfers between devices, extended(): lax.ppermute(tail, axis, [(i, (i + 1) % count) for i in range(ends)])  233 us
    ppermute x52, waiting for transfers between devices, extended(): lax.ppermute(head, axis, [((i + 1) % count, i) for i in range(ends)])  100 us
    ppermute x52, starting transfers between devices, extended(): lax.ppermute(head, axis, [((i + 1) % count, i) for i in range(ends)])  83.9 us
    ppermute x52, waiting for transfers between devices, extended(): lax.ppermute(tail, axis, [(i, (i + 1) % count) for i in range(ends)])  31.3 us
    dot_general x3, matrix products, apply_local(): jnp.einsum('dij,dxyjz->xyiz', face_matrices, stacked, precision=highest)  12.2 us
  transfers between devices with their start and end apart: 104, of which 58 were waited for; matrix products, arithmetic and copies ran while one was open for 0% of the time, Pallas kernels for 0%

commit v1 on v0

v1 whole, which is shorter than its diff:
```python
import functools

import jax
import jax.numpy as jnp
from jax import lax
from jax.experimental import pallas as pl
from jax.experimental.pallas import tpu as pltpu
from jax.sharding import PartitionSpec as P

NP = 64
EZ = 256
KC = 32
ITC = 24
SIDE = 4
COLS = SIDE * SIDE
PADS = SIDE + 2
damping = 0.8
highest = lax.Precision.HIGHEST
MESH = pl.DeviceIdType.MESH
f32, bf16 = jnp.float32, jnp.bfloat16


def halves(values):
    high = values.astype(bf16)
    return high, (values - high.astype(f32)).astype(bf16)


def iota(shape, axis):
    return lax.broadcasted_iota(jnp.int32, shape, axis)


def after(rows):
    return jnp.where(iota(rows.shape, 1) == 0, 0.0, pltpu.roll(rows, 1, 1))


def before(rows):
    last = rows.shape[1] - 1
    return jnp.where(iota(rows.shape, 1) == last, 0.0, pltpu.roll(rows, last, 1))


SOURCE = (
    lambda c: (SIDE - 1) * SIDE + c,
    lambda c: c,
    lambda c: c * SIDE + SIDE - 1,
    lambda c: c * SIDE,
)


def padded_slot(side, c):
    return (c + 1, (PADS - 1) * PADS + c + 1, (c + 1) * PADS, (c + 1) * PADS + PADS - 1)[side]


def exchange_kernel(
    gxn, gyn, zn,
    rhs_hbm, w_ref, agg_ref, e_ref, f_ref, r_ref, p_ref, shift_ref,
    base_ref, coef_ref, grhs_ref, gpiv_ref, aggh_ref,
    rhs_v, u1, u2, hal1, hal2, p1h, p1l, p2h, p2l, own_w, side_w,
    trow, tsend, thalo, asend, ahalo,
    s1a, r1a, s2a, r2a, s1b, r1b, s2b, r2b,
    load_sem, send1, recv1, send2, recv2, tsend_sem, trecv_sem, asend_sem, arecv_sem,
    gsem_a, gsem_b,
):
    gx, gy = lax.axis_index("gx"), lax.axis_index("gy")
    xg, zg = gx // zn, gx % zn
    xn = gxn // zn
    group = xn * gyn
    mine = xg * gyn + gy
    has = (gx > 0, gx < gxn - 1, gy > 0, gy < gyn - 1)
    sends = (has[1], has[0], has[3], has[2])
    target = ((gx + 1, gy), (gx - 1, gy), (gx, gy + 1), (gx, gy - 1))

    barrier = pltpu.get_barrier_semaphore()
    for s in (0, 1):
        @pl.when(sends[s])
        def _(s=s):
            pl.semaphore_signal(barrier, inc=1, device_id=target[s], device_id_type=MESH)

    def greet_plane(j, carry):
        @pl.when(j != mine)
        def _():
            pl.semaphore_signal(
                barrier, inc=1, device_id=((j // gyn) * zn + zg, j % gyn), device_id_type=MESH)
        return carry

    lax.fori_loop(0, group, greet_plane, 0)

    def greet_line(j, carry):
        @pl.when(j != zg)
        def _():
            pl.semaphore_signal(
                barrier, inc=1, device_id=(xg * zn + j, gy), device_id_type=MESH)
        return carry

    lax.fori_loop(0, zn, greet_line, 0)

    def load(x):
        return pltpu.make_async_copy(
            rhs_hbm.at[x], rhs_v.at[pl.ds(x * SIDE, SIDE)], load_sem.at[x])

    for x in (0, 3, 1, 2):
        load(x).start()

    same = iota((NP, NP), 0) == iota((NP, NP), 1)
    element = e_ref[...]
    on_diagonal = jnp.where(same, element, 0.0)
    diagonal = jnp.sum(on_diagonal, axis=1, keepdims=True)
    scale = damping / diagonal
    r_row = r_ref[...].reshape(1, NP)
    p_row = p_ref[...].reshape(1, NP)
    r_col = jnp.sum(jnp.where(same, r_row, 0.0), axis=1, keepdims=True)
    p_col = jnp.sum(jnp.where(same, p_row, 0.0), axis=1, keepdims=True)
    faces = [f_ref[d] for d in range(6)]
    scaled = [scale * face for face in faces]
    own_scaled = scale * element
    rows = [jnp.sum(r_col * m, axis=0, keepdims=True) for m in [element] + faces]
    rows.append(r_row * jnp.sum(on_diagonal, axis=0, keepdims=True) / damping)
    stacked = jnp.concatenate(
        [own_scaled, scaled[4], scaled[5]] + rows + [jnp.zeros((8, NP), f32)], axis=0)
    high, low = halves(stacked)
    own_w[:, 0:64] = high
    own_w[:, 64:128] = high
    own_w[:, 128:192] = low
    own_w[:, 192:256] = low
    for d in range(4):
        high, low = halves(scaled[d])
        side_w[0:64, d * 64:d * 64 + 64] = high
        side_w[64:128, d * 64:d * 64 + 64] = low

    for x in (0, 3, 1, 2):
        load(x).wait()

        def first(y, carry, x=x):
            col = x * SIDE + y
            value = rhs_v[col] * (1.0 / w_ref[x, pl.ds(y, 1), :]) * scale
            u1[col] = value
            slot = (x + 1) * PADS + y + 1
            p1h[slot], p1l[slot] = halves(value)
            return carry

        lax.fori_loop(0, SIDE, first, 0)

    asend[0] = agg_ref[SIDE - 1]
    asend[1] = agg_ref[0]
    for c in range(SIDE):
        asend[2, c:c + 1, :] = agg_ref[c, SIDE - 1:SIDE, :]
        asend[3, c:c + 1, :] = agg_ref[c, 0:1, :]

    in_group = iota((1, 128), 1) // KC == xg

    def spread(row):
        return jnp.where(in_group, jnp.concatenate([row] * 4, axis=1), 0.0)

    expected = group - 1 + zn - 1 + has[0].astype(jnp.int32) + has[1].astype(jnp.int32)
    pl.semaphore_wait(barrier, expected)

    def face(values, halo, send, recv, s, c):
        return pltpu.make_async_remote_copy(
            src_ref=values.at[SOURCE[s](c)], dst_ref=halo.at[s, c],
            send_sem=send.at[s, c], recv_sem=recv.at[s, c],
            device_id=target[s], device_id_type=MESH)

    face1 = functools.partial(face, u1, hal1, send1, recv1)
    face2 = functools.partial(face, u2, hal2, send2, recv2)

    def start(make, s, c):
        @pl.when(sends[s])
        def _():
            make(s, c).start()

    for c in range(SIDE):
        for s in range(4):
            start(face1, s, c)

    def small(values, halo, send, recv, s):
        return pltpu.make_async_remote_copy(
            src_ref=values.at[s], dst_ref=halo.at[s], send_sem=send.at[s], recv_sem=recv.at[s],
            device_id=target[s], device_id_type=MESH)

    labels = functools.partial(small, asend, ahalo, asend_sem, arecv_sem)
    scalars = functools.partial(small, tsend, thalo, tsend_sem, trecv_sem)

    for s in range(4):
        @pl.when(sends[s])
        def _(s=s):
            labels(s).start()

    def gather_first(s1, r1, sems, row):
        s1[...] = row
        r1[mine] = row

        def step(j, carry):
            @pl.when(j != mine)
            def _():
                pltpu.make_async_remote_copy(
                    src_ref=s1, dst_ref=r1.at[mine], send_sem=sems.at[0], recv_sem=sems.at[1],
                    device_id=((j // gyn) * zn + zg, j % gyn), device_id_type=MESH).start()
            return carry

        lax.fori_loop(0, group, step, 0)

    def wait_bytes(ref, count, sem):
        part = ref.at[pl.ds(0, count)]
        pltpu.make_async_copy(part, part, sem).wait()

    def gather_second(r1, s2, r2, sems):
        wait_bytes(r1, group - 1, sems.at[1])
        if gyn < 8:
            s2[...] = jnp.zeros_like(s2)
        for b in range(gyn):
            s2[b:b + 1, :] = sum(r1[q * gyn + b] for q in range(xn))
        r2[zg] = s2[...]

        def step(j, carry):
            @pl.when(j != zg)
            def _():
                pltpu.make_async_remote_copy(
                    src_ref=s2, dst_ref=r2.at[zg], send_sem=sems.at[2], recv_sem=sems.at[3],
                    device_id=(xg * zn + j, gy), device_id_type=MESH).start()
            return carry

        lax.fori_loop(0, zn, step, 0)

    def gather_third(r1, r2, sems, out):
        wait_bytes(r2, zn - 1, sems.at[3])
        out[...] = r2[...]
        wait_bytes(r1, group - 1, sems.at[0])
        wait_bytes(r2, zn - 1, sems.at[2])

    gather_first(s1a, r1a, gsem_a, spread(1.0 / (6.0 + shift_ref[0])))

    nothing = jnp.zeros((NP, EZ), bf16)
    for s in range(4):
        @pl.when(jnp.logical_not(has[s]))
        def _(s=s):
            thalo[s] = jnp.zeros((SIDE, EZ), f32)
            ahalo[s] = jnp.zeros((SIDE, EZ), jnp.int32)
            for c in range(SIDE):
                slot = padded_slot(s, c)
                p1h[slot] = nothing
                p1l[slot] = nothing
                p2h[slot] = nothing
                p2l[slot] = nothing

    own_matrix = own_w
    side_matrix = side_w

    def own_part(high_ref, low_ref, slot):
        high, low = high_ref[slot], low_ref[slot]
        g = jnp.dot(own_matrix[...], jnp.concatenate([high, low, high, low], axis=0),
                    preferred_element_type=f32)
        return g[0:64] - after(g[64:128]) - before(g[128:192]), g[192:200]

    def side_part(high_ref, low_ref, slot):
        around = (slot - PADS, slot + PADS, slot - 1, slot + 1)
        high = jnp.concatenate([high_ref[s] for s in around], axis=0)
        low = jnp.concatenate([low_ref[s] for s in around], axis=0)
        both = jnp.dot(side_matrix[...], high, preferred_element_type=f32)
        return both[0:64] + both[64:128] + jnp.dot(
            side_matrix[0:64, :], low, preferred_element_type=f32)

    def second(x, y):
        col, slot = x * SIDE + y, (x + 1) * PADS + y + 1
        before_it = u1[col]
        own, from_u1 = own_part(p1h, p1l, slot)
        value = 2.0 * before_it - own + side_part(p1h, p1l, slot)
        u2[col] = value
        p2h[slot], p2l[slot] = halves(value)
        own, from_u2 = own_part(p2h, p2l, slot)
        base_ref[col] = value + before_it - own
        total = from_u1[7:8] - from_u2[0:1] + after(from_u2[5:6]) + before(from_u2[6:7])
        trow[col] = jnp.where(iota((8, EZ), 0) == 0, total, from_u2)

    def arrive(make, halo, high_ref, low_ref, s, c):
        @pl.when(has[s])
        def _():
            make(s, c).wait_recv()
            slot = padded_slot(s, c)
            high_ref[slot], low_ref[slot] = halves(halo[s, c])

    arrive1 = functools.partial(arrive, face1, hal1, p1h, p1l)
    arrive2 = functools.partial(arrive, face2, hal2, p2h, p2l)

    def interior(i, carry):
        second(1, i + 1)
        second(2, i + 1)
        return carry

    lax.fori_loop(0, 2, interior, 0)
    for c in range(SIDE):
        for s in (2, 3):
            arrive1(s, c)
    gather_second(r1a, s2a, r2a, gsem_a)

    def side_y(i, carry):
        second(i + 1, 0)
        second(i + 1, SIDE - 1)
        return carry

    lax.fori_loop(0, 2, side_y, 0)
    for c in (1, 2):
        for s in (2, 3):
            start(face2, s, c)
    for c in range(SIDE):
        arrive1(0, c)
        arrive1(1, c)
        second(0, c)
        second(SIDE - 1, c)
        start(face2, 0, c)
        start(face2, 1, c)
        if c in (0, SIDE - 1):
            s = 3 if c == 0 else 2
            start(face2, s, 0)
            start(face2, s, SIDE - 1)

    for s in range(4):
        for c in range(SIDE):
            tsend[s, c:c + 1, :] = trow[SOURCE[s](c), s + 1:s + 2, :]

        @pl.when(sends[s])
        def _(s=s):
            scalars(s).start()

    def last(x, y):
        col, slot = x * SIDE + y, (x + 1) * PADS + y + 1
        base_ref[col] += side_part(p2h, p2l, slot)

    def last_interior(i, carry):
        last(1, i + 1)
        last(2, i + 1)
        return carry

    lax.fori_loop(0, 2, last_interior, 0)

    for s in range(4):
        @pl.when(has[s])
        def _(s=s):
            scalars(s).wait_recv()

    levels = iota((KC, EZ), 0)
    total = jnp.zeros((KC, EZ), f32)
    for x in range(SIDE):
        for y in range(SIDE):
            col = x * SIDE + y
            row = trow[col, 0:1, :]
            row += trow[col - SIDE, 1:2, :] if x > 0 else thalo[0, y:y + 1, :]
            row += trow[col + SIDE, 2:3, :] if x < SIDE - 1 else thalo[1, y:y + 1, :]
            row += trow[col - 1, 3:4, :] if y > 0 else thalo[2, x:x + 1, :]
            row += trow[col + 1, 4:5, :] if y < SIDE - 1 else thalo[3, x:x + 1, :]
            row = row * w_ref[x, y:y + 1, :]
            total += jnp.where(agg_ref[x, y:y + 1, :] == levels, row, 0.0)
    sums = lax.dot_general(
        jnp.ones((8, EZ), f32), jnp.concatenate([total] * 4, axis=0),
        (((1,), (1,)), ((), ())), precision=highest, preferred_element_type=f32)
    gather_first(s1b, r1b, gsem_b, jnp.where(in_group, sums[0:1], 0.0))

    for c in range(SIDE):
        for s in (2, 3):
            arrive2(s, c)

    def last_y(i, carry):
        last(i + 1, 0)
        last(i + 1, SIDE - 1)
        return carry

    lax.fori_loop(0, 2, last_y, 0)
    gather_second(r1b, s2b, r2b, gsem_b)

    gains = [jnp.sum(m * p_row, axis=1, keepdims=True) for m in scaled]
    own_gain = p_col - jnp.sum(own_scaled * p_row, axis=1, keepdims=True)
    lane = iota((NP, 256), 1)
    at = lane % 64

    def coefficients(col, carry):
        x, y = col // SIDE, col % SIDE
        places = (
            jnp.where(x > 0, col - SIDE, COLS + y),
            jnp.where(x < SIDE - 1, col + SIDE, COLS + SIDE + y),
            jnp.where(y > 0, col - 1, COLS + 2 * SIDE + x),
            jnp.where(y < SIDE - 1, col + 1, COLS + 3 * SIDE + x),
            2 * COLS + col,
            3 * COLS + col,
        )
        matrix = jnp.where(at == col, own_gain, 0.0)
        for d in range(6):
            matrix = jnp.where(at == places[d], gains[d], matrix)
        high, low = halves(matrix)
        coef_ref[col] = jnp.where(lane < 128, high.astype(f32), low.astype(f32)).astype(bf16)
        return carry

    lax.fori_loop(0, COLS, coefficients, 0)

    for c in range(SIDE):
        arrive2(0, c)
        arrive2(1, c)
        last(0, c)
        last(SIDE - 1, c)

    for s in range(4):
        @pl.when(has[s])
        def _(s=s):
            labels(s).wait_recv()
    aggh_ref[...] = ahalo[...]
    gather_third(r1a, r2a, gsem_a, gpiv_ref)
    gather_third(r1b, r2b, gsem_b, grhs_ref)

    for s in range(4):
        @pl.when(sends[s])
        def _(s=s):
            labels(s).wait_send()
            scalars(s).wait_send()
            for c in range(SIDE):
                face1(s, c).wait_send()
                face2(s, c).wait_send()


def finish_kernel(
    gxn, gyn, zn,
    base_ref, coef_ref, grhs_ref, gpiv_ref, aggh_ref, agg_ref,
    out_hbm, corr_ref,
    out_v, coarse, labels, lifted, out_sem,
):
    gx, gy = lax.axis_index("gx"), lax.axis_index("gy")
    lane, sub = iota((8, 128), 1), iota((8, 128), 0)
    level = lane % KC

    rhs = [grhs_ref[i] for i in range(zn)]
    pivot = [gpiv_ref[i] for i in range(zn)]

    def sweep(repeat, now):
        new = []
        wrap_low = jnp.where(lane < KC, 0.0, pltpu.roll(now[zn - 1], KC, 1))
        wrap_high = jnp.where(lane >= 128 - KC, 0.0, pltpu.roll(now[0], 128 - KC, 1))
        for i in range(zn):
            value = now[i]
            total = rhs[i] + (now[i - 1] if i > 0 else wrap_low)
            total += now[i + 1] if i < zn - 1 else wrap_high
            total += jnp.where(sub == 0, 0.0, pltpu.roll(value, 1, 0))
            total += jnp.where(sub == 7, 0.0, pltpu.roll(value, 7, 0))
            total += jnp.where(level == 0, 0.0, pltpu.roll(value, 1, 1))
            total += jnp.where(level == KC - 1, 0.0, pltpu.roll(value, 127, 1))
            new.append(total * pivot[i])
        return tuple(new)

    now = lax.fori_loop(0, ITC - 1, sweep, tuple(a * b for a, b in zip(rhs, pivot)))
    for i in range(zn):
        coarse[i] = now[i]

    def table(ax, ay):
        shifted = ax + zn
        value = coarse[shifted % zn]
        value = jnp.where((sub == ay) & (lane // KC == shifted // zn - 1), value, 0.0)
        row = jnp.sum(value, axis=0, keepdims=True)
        row = row + pltpu.roll(row, 64, 1)
        return row + pltpu.roll(row, 32, 1)

    own = table(gx, gy)
    corr_ref[0] = own[:, :KC]
    sides = [table(gx - 1, gy), table(gx + 1, gy), table(gx, gy - 1), table(gx, gy + 1)]
    tables = [jnp.broadcast_to(own, (8, 128))] * 2 + [
        jnp.where(sub < 4, sides[0], sides[1]), jnp.where(sub < 4, sides[2], sides[3])]
    for x in range(SIDE):
        labels[x * SIDE:(x + 1) * SIDE, :] = agg_ref[x]
        labels[COLS + x * SIDE:COLS + (x + 1) * SIDE, :] = aggh_ref[x]
    for i in range(4):
        for half in range(2):
            picked = labels[i * 8:i * 8 + 8, half * 128:half * 128 + 128]
            lifted[i * 8:i * 8 + 8, half * 128:half * 128 + 128] = jnp.take_along_axis(
                tables[i], picked, axis=1)
    lifted[32:48, :] = after(lifted[0:16, :])
    lifted[48:64, :] = before(lifted[0:16, :])
    high, low = halves(lifted[...])
    around = jnp.concatenate([high, low, high, low], axis=0)

    def store(x):
        return pltpu.make_async_copy(
            out_v.at[pl.ds(x * SIDE, SIDE)], out_hbm.at[x], out_sem.at[x])

    for x in range(SIDE):
        for y in range(SIDE):
            col = x * SIDE + y
            out_v[col] = base_ref[col] + jnp.dot(coef_ref[col], around, preferred_element_type=f32)
        store(x).start()
    for x in range(SIDE):
        store(x).wait()


def body(gxn, gyn, zn, right_side, diffusivity, agglomerate, element_matrix, face_matrices,
         restriction, prolongation, coarse_shift):
    group = gxn // zn * gyn
    vmem = pl.BlockSpec(memory_space=pltpu.VMEM)
    hbm = pl.BlockSpec(memory_space=pl.ANY)
    dma = pltpu.SemaphoreType.DMA
    field = pltpu.VMEM((COLS, NP, EZ), f32)
    halo = pltpu.VMEM((4, SIDE, NP, EZ), f32)
    parts = pltpu.VMEM((PADS * PADS, NP, EZ), bf16)
    gather = [
        pltpu.VMEM((1, 128), f32),
        pltpu.VMEM((group, 1, 128), f32),
        pltpu.VMEM((8, 128), f32),
        pltpu.VMEM((zn, 8, 128), f32),
    ]
    side_rows = pltpu.VMEM((4, SIDE, EZ), f32)
    side_labels = pltpu.VMEM((4, SIDE, EZ), jnp.int32)
    base, coef, grhs, gpiv, aggh = pl.pallas_call(
        functools.partial(exchange_kernel, gxn, gyn, zn),
        out_shape=(
            jax.ShapeDtypeStruct((COLS, NP, EZ), f32),
            jax.ShapeDtypeStruct((COLS, NP, 256), bf16),
            jax.ShapeDtypeStruct((zn, 8, 128), f32),
            jax.ShapeDtypeStruct((zn, 8, 128), f32),
            jax.ShapeDtypeStruct((4, SIDE, EZ), jnp.int32),
        ),
        in_specs=[hbm] + [vmem] * 7,
        out_specs=(vmem,) * 5,
        scratch_shapes=[
            field, field, field, halo, halo, parts, parts, parts, parts,
            pltpu.VMEM((208, 256), bf16), pltpu.VMEM((128, 256), bf16),
            pltpu.VMEM((COLS, 8, EZ), f32), side_rows, side_rows, side_labels, side_labels,
            *gather, *gather,
            dma((SIDE,)), dma((4, SIDE)), dma((4, SIDE)), dma((4, SIDE)), dma((4, SIDE)),
            dma((4,)), dma((4,)), dma((4,)), dma((4,)), dma((4,)), dma((4,)),
        ],
        compiler_params=pltpu.CompilerParams(
            collective_id=0, has_side_effects=True, vmem_limit_bytes=40 * 2**20),
        name="exchange",
    )(right_side, diffusivity, agglomerate, element_matrix, face_matrices, restriction,
      prolongation, coarse_shift)
    return pl.pallas_call(
        functools.partial(finish_kernel, gxn, gyn, zn),
        out_shape=(
            jax.ShapeDtypeStruct((SIDE, SIDE, NP, EZ), f32),
            jax.ShapeDtypeStruct((1, 1, KC), f32),
        ),
        in_specs=[vmem] * 6,
        out_specs=(hbm, vmem),
        scratch_shapes=[
            field, pltpu.VMEM((zn, 8, 128), f32), pltpu.VMEM((32, EZ), jnp.int32),
            pltpu.VMEM((64, EZ), f32), dma((SIDE,)),
        ],
        compiler_params=pltpu.CompilerParams(vmem_limit_bytes=20 * 2**20),
        name="finish",
    )(base, coef, grhs, gpiv, aggh, agglomerate)


def solution(mesh):
    gxn, gyn = mesh.shape["gx"], mesh.shape["gy"]
    return jax.shard_map(
        functools.partial(body, gxn, gyn, max(1, gxn // 4)),
        mesh=mesh,
        in_specs=(
            P("gx", "gy", None, None),
            P("gx", "gy", None),
            P("gx", "gy", None),
            P(),
            P(),
            P(),
            P(),
            P("gx", "gy", None),
        ),
        out_specs=(P("gx", "gy", None, None), P("gx", "gy", None)),
        check_vma=False,
    )
```

time: 485 us -> 50.2 us (0.10); the launches traced: 479 us -> 49.8 us
  starting transfers between devices: 317 us -> 0 us
  waiting for transfers between devices: 132 us -> 0 us
  Pallas kernels: 0 us -> 42.8 us
  matrix products: 18.5 us -> 0 us
  other arithmetic: 4.88 us -> 0 us
    ppermute x104 -> x0, starting transfers between devices: 317 us -> none  [the longest x52 233 us: extended(): lax.ppermute(tail, axis, [(i, (i + 1) % count) for i in range(ends)])]
    ppermute x104 -> x0, waiting for transfers between devices: 132 us -> none  [the longest x52 100 us: extended(): lax.ppermute(head, axis, [((i + 1) % count, i) for i in range(ends)])]
    pallas_call x0 -> x2, Pallas kernels: none -> 42.8 us  [the longest x1 38.8 us: body(): pl.pallas_call(functools.partial(exchange_kernel, gxn, gyn, zn), out_shap...]
    dot_general x9 -> x0, matrix products: 18.5 us -> none  [the longest x3 12.2 us: apply_local(): jnp.einsum('dij,dxyjz->xyiz', face_matrices, stacked, precision=highest)]
    unnamed x21 -> x16, local copies, waits for them, and re-layouts: 1.07 us -> 6.3 us
  transfers between devices with their start and end apart: 104 -> 0, of which waited for: 58 -> 0; matrix products, arithmetic and copies ran while one was open for 0% -> 0% of each run, Pallas kernels for 0% -> 0%
where the time goes in v1:
time: 50.2 us; the launch traced here: 49.8 us
  Pallas kernels  42.8 us (85%)
  local copies, waits for them, and re-layouts  6.3 us (13%)
  between operations  0.66 us (1%)
    pallas_call x1, Pallas kernels, body(): pl.pallas_call(functools.partial(exchange_kernel, gxn, gyn, zn), out_shap...  38.8 us
    unnamed x16, local copies, waits for them, and re-layouts  6.3 us
    pallas_call x1, Pallas kernels, body(): pl.pallas_call(functools.partial(finish_kernel, gxn, gyn, zn), out_shape=...  4.09 us

profile of v1, /device:TPU:1, one launch (start us, length us, event | category | flops | bytes accessed | tf_op | source)
XLA Modules:
  0.0 49.8 jit_solution(7624323672312007575)
XLA Ops:
  0.6 0.0 copy-start
  0.6 1.2 %copy-done = f32[4,4,64,256]{3,2,1,0:T(8,128)S(1)} copy-done((f32[4,4,64,256]{3,2,1,0:T(8,128)S(1)}, f32[4,4,64,256]{3,2,1,0:T(8,128)}, u32[]{:S(2)}) %copy-start) | copy-done | bytes 1048600
  1.9 0.0 copy-start.1
  1.9 0.9 %copy-done.1 = f32[6,64,64]{2,1,0:T(8,128)S(1)} copy-done((f32[6,64,64]{2,1,0:T(8,128)S(1)}, f32[6,64,64]{2,1,0:T(8,128)}, u32[]{:S(2)}) %copy-start.1) | copy-done | bytes 98328
  2.8 0.0 copy-start.2
  2.8 0.7 %copy-done.2 = s32[4,4,256]{2,1,0:T(4,128)S(1)} copy-done((s32[4,4,256]{2,1,0:T(4,128)S(1)}, s32[4,4,256]{2,1,0:T(4,128)}, u32[]{:S(2)}) %copy-start.2) | copy-done | bytes 16408
  3.5 0.0 copy-start.3
  3.5 0.8 %copy-done.3 = f32[64,64]{1,0:T(8,128)S(1)} copy-done((f32[64,64]{1,0:T(8,128)S(1)}, f32[64,64]{1,0:T(8,128)}, u32[]{:S(2)}) %copy-start.3) | copy-done | bytes 16408
  4.3 0.0 copy-start.4
  4.3 0.7 %copy-done.4 = f32[4,4,256]{2,1,0:T(4,128)S(1)} copy-done((f32[4,4,256]{2,1,0:T(4,128)S(1)}, f32[4,4,256]{2,1,0:T(4,128)}, u32[]{:S(2)}) %copy-start.4) | copy-done | bytes 16408
  5.0 0.0 copy-start.5
  5.0 0.7 %copy-done.5 = f32[64]{0:T(128)S(1)} copy-done((f32[64]{0:T(128)S(1)}, f32[64]{0:T(128)}, u32[]{:S(2)}) %copy-start.5) | copy-done | bytes 280
  5.6 0.0 copy-start.6
  5.6 0.7 %copy-done.6 = f32[64]{0:T(128)S(1)} copy-done((f32[64]{0:T(128)S(1)}, f32[64]{0:T(128)}, u32[]{:S(2)}) %copy-start.6) | copy-done | bytes 280
  6.3 0.0 copy-start.7
  6.3 0.7 %copy-done.7 = f32[1,1,32]{2,1,0:T(1,128)S(1)} copy-done((f32[1,1,32]{2,1,0:T(1,128)S(1)}, f32[1,1,32]{2,1,0:T(1,128)}, u32[]{:S(2)}) %copy-start.7) | copy-done | bytes 152
  6.9 38.8 %exchange.1 = (f32[16,64,256]{2,1,0:T(8,128)S(1)}, bf16[16,64,256]{2,1,0:T(8,128)(2,1)S(1)}, f32[8,8,128]{2,1,0:T(8,128)S(1)}, f32[8,8,128]{2,1,0:T(8,128)S(1)}, s32[4,4,256]{2,1,0:T(4,128)S(1)}) custom-call(f32[4,4,64,256]{3,2,1,0:T(8,128)S(1)} %copy-done, f32[4,4,256]{2,1,0:T(4,128)S(1)} %copy-done.4, s32[4,4,256]{2,1,0:T(4,128)S(1)} %copy-done.2, ...), custom_call_target="tpu_custom_call" | custom-call | tf_op jit(solution)/shard_map/exchange/pallas_call | solution.py:504
  45.7 4.1 %finish.1 = (f32[4,4,64,256]{3,2,1,0:T(8,128)}, f32[1,1,32]{2,1,0:T(1,128)}) custom-call(f32[16,64,256]{2,1,0:T(8,128)S(1)} %get-tuple-element.7.base_ref, bf16[16,64,256]{2,1,0:T(8,128)(2,1)S(1)} %get-tuple-element.8.coef_ref, f32[8,8,128]{2,1,0:T(8,128)S(1)} %get-tuple-element.9.grhs_ref, f32[8,8,128]{2,1,0:T(8,128)S(1)} %get-tuple-element.10.gpiv_ref, ...), custom_call_target="tpu_custom_call" | custom-call | tf_op jit(solution)/shard_map/finish/pallas_call | solution.py:528
Async XLA Ops:
  0.6 1.2 %copy-start = (f32[4,4,64,256]{3,2,1,0:T(8,128)S(1)}, f32[4,4,64,256]{3,2,1,0:T(8,128)}, u32[]{:S(2)}) copy-start(f32[4,4,64,256]{3,2,1,0:T(8,128)} %rhs_hbm.1) | copy-start | bytes 3145732
  1.9 0.9 %copy-start.1 = (f32[6,64,64]{2,1,0:T(8,128)S(1)}, f32[6,64,64]{2,1,0:T(8,128)}, u32[]{:S(2)}) copy-start(f32[6,64,64]{2,1,0:T(8,128)} %f_ref.1) | copy-start | bytes 294916
  2.8 0.7 %copy-start.2 = (s32[4,4,256]{2,1,0:T(4,128)S(1)}, s32[4,4,256]{2,1,0:T(4,128)}, u32[]{:S(2)}) copy-start(s32[4,4,256]{2,1,0:T(4,128)} %agg_ref.3) | copy-start | bytes 49156
  3.5 0.8 %copy-start.3 = (f32[64,64]{1,0:T(8,128)S(1)}, f32[64,64]{1,0:T(8,128)}, u32[]{:S(2)}) copy-start(f32[64,64]{1,0:T(8,128)} %e_ref.1) | copy-start | bytes 49156
  4.3 0.7 %copy-start.4 = (f32[4,4,256]{2,1,0:T(4,128)S(1)}, f32[4,4,256]{2,1,0:T(4,128)}, u32[]{:S(2)}) copy-start(f32[4,4,256]{2,1,0:T(4,128)} %w_ref.1) | copy-start | bytes 49156
  5.0 0.7 %copy-start.5 = (f32[64]{0:T(128)S(1)}, f32[64]{0:T(128)}, u32[]{:S(2)}) copy-start(f32[64]{0:T(128)} %r_ref.1) | copy-start | bytes 772
  5.6 0.7 %copy-start.6 = (f32[64]{0:T(128)S(1)}, f32[64]{0:T(128)}, u32[]{:S(2)}) copy-start(f32[64]{0:T(128)} %p_ref.1) | copy-start | bytes 772
  6.3 0.7 %copy-start.7 = (f32[1,1,32]{2,1,0:T(1,128)S(1)}, f32[1,1,32]{2,1,0:T(1,128)}, u32[]{:S(2)}) copy-start(f32[1,1,32]{2,1,0:T(1,128)} %shift_ref.1) | copy-start | bytes 388

commit v2 on v1

--- a/solution.py
+++ b/solution.py
@@ -52,12 +52,12 @@
 
 def exchange_kernel(
     gxn, gyn, zn,
-    rhs_hbm, w_ref, agg_ref, e_ref, f_ref, r_ref, p_ref, shift_ref,
-    base_ref, coef_ref, grhs_ref, gpiv_ref, aggh_ref,
-    rhs_v, u1, u2, hal1, hal2, p1h, p1l, p2h, p2l, own_w, side_w,
+    rhs_hbm, w_hbm, agg_hbm, e_hbm, f_hbm, r_hbm, p_hbm, shift_hbm,
+    base_ref, coef_ref, grhs_ref, gpiv_ref, labels_ref,
+    w_ref, agg_ref, e_ref, f_ref, r_ref, p_ref, shift_ref, rhs_v, u1, u2, hal1, hal2, p1h, p1l, p2h, p2l, own_w, side_w,
     trow, tsend, thalo, asend, ahalo,
     s1a, r1a, s2a, r2a, s1b, r1b, s2b, r2b,
-    load_sem, send1, recv1, send2, recv2, tsend_sem, trecv_sem, asend_sem, arecv_sem,
+    small_sem, load_sem, send1, recv1, send2, recv2, tsend_sem, trecv_sem, asend_sem, arecv_sem,
     gsem_a, gsem_b,
 ):
     gx, gy = lax.axis_index("gx"), lax.axis_index("gy")
@@ -69,6 +69,19 @@
     sends = (has[1], has[0], has[3], has[2])
     target = ((gx + 1, gy), (gx - 1, gy), (gx, gy + 1), (gx, gy - 1))
 
+    def load(x):
+        return pltpu.make_async_copy(
+            rhs_hbm.at[x], rhs_v.at[pl.ds(x * SIDE, SIDE)], load_sem.at[x])
+
+    inputs = [
+        pltpu.make_async_copy(a, b, small_sem.at[i]) for i, (a, b) in enumerate((
+            (e_hbm, e_ref), (f_hbm, f_ref), (r_hbm, r_ref), (p_hbm, p_ref), (w_hbm, w_ref),
+            (shift_hbm, shift_ref), (agg_hbm, agg_ref)))]
+    for copy in inputs:
+        copy.start()
+    for x in (0, 3, 1, 2):
+        load(x).start()
+
     barrier = pltpu.get_barrier_semaphore()
     for s in (0, 1):
         @pl.when(sends[s])
@@ -93,12 +106,8 @@
 
     lax.fori_loop(0, zn, greet_line, 0)
 
-    def load(x):
-        return pltpu.make_async_copy(
-            rhs_hbm.at[x], rhs_v.at[pl.ds(x * SIDE, SIDE)], load_sem.at[x])
-
-    for x in (0, 3, 1, 2):
-        load(x).start()
+    for copy in inputs:
+        copy.wait()
 
     same = iota((NP, NP), 0) == iota((NP, NP), 1)
     element = e_ref[...]
@@ -139,6 +148,8 @@
 
         lax.fori_loop(0, SIDE, first, 0)
 
+    for x in range(SIDE):
+        labels_ref[x * SIDE:(x + 1) * SIDE, :] = agg_ref[x]
     asend[0] = agg_ref[SIDE - 1]
     asend[1] = agg_ref[0]
     for c in range(SIDE):
@@ -399,7 +410,8 @@
         @pl.when(has[s])
         def _(s=s):
             labels(s).wait_recv()
-    aggh_ref[...] = ahalo[...]
+    for s in range(4):
+        labels_ref[COLS + s * SIDE:COLS + (s + 1) * SIDE, :] = ahalo[s]
     gather_third(r1a, r2a, gsem_a, gpiv_ref)
     gather_third(r1b, r2b, gsem_b, grhs_ref)
 
@@ -415,9 +427,9 @@
 
 def finish_kernel(
     gxn, gyn, zn,
-    base_ref, coef_ref, grhs_ref, gpiv_ref, aggh_ref, agg_ref,
+    base_ref, coef_ref, grhs_ref, gpiv_ref, labels,
     out_hbm, corr_ref,
-    out_v, coarse, labels, lifted, out_sem,
+    out_v, coarse, lifted, out_sem,
 ):
     gx, gy = lax.axis_index("gx"), lax.axis_index("gy")
     lane, sub = iota((8, 128), 1), iota((8, 128), 0)
@@ -458,9 +470,6 @@
     sides = [table(gx - 1, gy), table(gx + 1, gy), table(gx, gy - 1), table(gx, gy + 1)]
     tables = [jnp.broadcast_to(own, (8, 128))] * 2 + [
         jnp.where(sub < 4, sides[0], sides[1]), jnp.where(sub < 4, sides[2], sides[3])]
-    for x in range(SIDE):
-        labels[x * SIDE:(x + 1) * SIDE, :] = agg_ref[x]
-        labels[COLS + x * SIDE:COLS + (x + 1) * SIDE, :] = aggh_ref[x]
     for i in range(4):
         for half in range(2):
             picked = labels[i * 8:i * 8 + 8, half * 128:half * 128 + 128]
@@ -501,45 +510,48 @@
     ]
     side_rows = pltpu.VMEM((4, SIDE, EZ), f32)
     side_labels = pltpu.VMEM((4, SIDE, EZ), jnp.int32)
-    base, coef, grhs, gpiv, aggh = pl.pallas_call(
+    base, coef, grhs, gpiv, labels = pl.pallas_call(
         functools.partial(exchange_kernel, gxn, gyn, zn),
         out_shape=(
             jax.ShapeDtypeStruct((COLS, NP, EZ), f32),
             jax.ShapeDtypeStruct((COLS, NP, 256), bf16),
             jax.ShapeDtypeStruct((zn, 8, 128), f32),
             jax.ShapeDtypeStruct((zn, 8, 128), f32),
-            jax.ShapeDtypeStruct((4, SIDE, EZ), jnp.int32),
+            jax.ShapeDtypeStruct((2 * COLS, EZ), jnp.int32),
         ),
-        in_specs=[hbm] + [vmem] * 7,
+        in_specs=[pl.BlockSpec(memory_space=pltpu.HBM)] * 8,
         out_specs=(vmem,) * 5,
         scratch_shapes=[
+            pltpu.VMEM((SIDE, SIDE, EZ), f32), pltpu.VMEM((SIDE, SIDE, EZ), jnp.int32),
+            pltpu.VMEM((NP, NP), f32), pltpu.VMEM((6, NP, NP), f32), pltpu.VMEM((NP,), f32),
+            pltpu.VMEM((NP,), f32), pltpu.VMEM((1, 1, KC), f32),
             field, field, field, halo, halo, parts, parts, parts, parts,
             pltpu.VMEM((208, 256), bf16), pltpu.VMEM((128, 256), bf16),
             pltpu.VMEM((COLS, 8, EZ), f32), side_rows, side_rows, side_labels, side_labels,
             *gather, *gather,
-            dma((SIDE,)), dma((4, SIDE)), dma((4, SIDE)), dma((4, SIDE)), dma((4, SIDE)),
+            dma((7,)), dma((SIDE,)), dma((4, SIDE)), dma((4, SIDE)), dma((4, SIDE)), dma((4, SIDE)),
             dma((4,)), dma((4,)), dma((4,)), dma((4,)), dma((4,)), dma((4,)),
         ],
         compiler_params=pltpu.CompilerParams(
             collective_id=0, has_side_effects=True, vmem_limit_bytes=40 * 2**20),
         name="exchange",
-    )(right_side, diffusivity, agglomerate, element_matrix, face_matrices, restriction,
-      prolongation, coarse_shift)
+    )(*[pltpu.with_memory_space_constraint(value, pltpu.HBM) for value in (
+        right_side, diffusivity, agglomerate, element_matrix, face_matrices, restriction,
+        prolongation, coarse_shift)])
     return pl.pallas_call(
         functools.partial(finish_kernel, gxn, gyn, zn),
         out_shape=(
             jax.ShapeDtypeStruct((SIDE, SIDE, NP, EZ), f32),
             jax.ShapeDtypeStruct((1, 1, KC), f32),
         ),
-        in_specs=[vmem] * 6,
+        in_specs=[vmem] * 5,
         out_specs=(hbm, vmem),
         scratch_shapes=[
-            field, pltpu.VMEM((zn, 8, 128), f32), pltpu.VMEM((32, EZ), jnp.int32),
-            pltpu.VMEM((64, EZ), f32), dma((SIDE,)),
+            field, pltpu.VMEM((zn, 8, 128), f32), pltpu.VMEM((64, EZ), f32), dma((SIDE,)),
         ],
         compiler_params=pltpu.CompilerParams(vmem_limit_bytes=20 * 2**20),
         name="finish",
-    )(base, coef, grhs, gpiv, aggh, agglomerate)
+    )(base, coef, grhs, gpiv, labels)
 
 
 def solution(mesh):

time: 50.2 us -> 44.1 us (0.88)
  local copies, waits for them, and re-layouts: 6.3 us -> 0 us
  Pallas kernels: 42.8 us -> 43.4 us
    unnamed x16 -> x0, local copies, waits for them, and re-layouts: 6.3 us -> none
    pallas_call x1, Pallas kernels: 38.8 us -> 39.3 us  [body(): pl.pallas_call(functools.partial(exchange_kernel, gxn, gyn, zn), out_shap...]
where the time goes in v2:
time: 44.1 us; the launch traced here: 44 us
  Pallas kernels  43.4 us (98%)
  between operations  0.64 us (1%)
    pallas_call x1, Pallas kernels, body(): pl.pallas_call(functools.partial(exchange_kernel, gxn, gyn, zn), out_shap...  39.3 us
    pallas_call x1, Pallas kernels, body(): pl.pallas_call(functools.partial(finish_kernel, gxn, gyn, zn), out_shape=...  4.08 us

profile of v2, /device:TPU:1, one launch (start us, length us, event | category | flops | bytes accessed | tf_op | source)
XLA Modules:
  0.0 44.0 jit_solution(2090545884088202260)
XLA Ops:
  0.6 39.3 %exchange.1 = (f32[16,64,256]{2,1,0:T(8,128)S(1)}, bf16[16,64,256]{2,1,0:T(8,128)(2,1)S(1)}, f32[8,8,128]{2,1,0:T(8,128)S(1)}, f32[8,8,128]{2,1,0:T(8,128)S(1)}, s32[32,256]{1,0:T(8,128)S(1)}) custom-call(f32[4,4,64,256]{3,2,1,0:T(8,128)} %rhs_hbm.1, f32[4,4,256]{2,1,0:T(4,128)} %w_hbm.1, s32[4,4,256]{2,1,0:T(4,128)} %agg_hbm.1, f32[64,64]{1,0:T(8,128)} %e_hbm.1, ...), custom_call_target="tpu_custom_call" | custom-call | tf_op jit(solution)/shard_map/exchange/pallas_call | solution.py:513
  39.9 4.1 %finish.1 = (f32[4,4,64,256]{3,2,1,0:T(8,128)}, f32[1,1,32]{2,1,0:T(1,128)}) custom-call(f32[16,64,256]{2,1,0:T(8,128)S(1)} %get-tuple-element.7.base_ref, bf16[16,64,256]{2,1,0:T(8,128)(2,1)S(1)} %get-tuple-element.8.coef_ref, f32[8,8,128]{2,1,0:T(8,128)S(1)} %get-tuple-element.9.grhs_ref, f32[8,8,128]{2,1,0:T(8,128)S(1)} %get-tuple-element.10.gpiv_ref, ...), custom_call_target="tpu_custom_call" | custom-call | tf_op jit(solution)/shard_map/finish/pallas_call | solution.py:541

commit v3 on v2

--- a/solution.py
+++ b/solution.py
@@ -54,11 +54,11 @@
     gxn, gyn, zn,
     rhs_hbm, w_hbm, agg_hbm, e_hbm, f_hbm, r_hbm, p_hbm, shift_hbm,
     base_ref, coef_ref, grhs_ref, gpiv_ref, labels_ref,
-    w_ref, agg_ref, e_ref, f_ref, r_ref, p_ref, shift_ref, rhs_v, u1, u2, hal1, hal2, p1h, p1l, p2h, p2l, own_w, side_w,
-    trow, tsend, thalo, asend, ahalo,
+    w_ref, agg_ref, e_ref, f_ref, r_ref, p_ref, shift_ref, rhs_v, u1, u2, hal1, hal2, p1h, p1l, p2h, p2l, own_w, side_w, path_w,
+    field, qsend, qhalo, trow, tsend, thalo, asend, ahalo,
     s1a, r1a, s2a, r2a, s1b, r1b, s2b, r2b,
     small_sem, load_sem, send1, recv1, send2, recv2, tsend_sem, trecv_sem, asend_sem, arecv_sem,
-    gsem_a, gsem_b,
+    gsem_a, gsem_b, qsend_sem, qrecv_sem,
 ):
     gx, gy = lax.axis_index("gx"), lax.axis_index("gy")
     xg, zg = gx // zn, gx % zn
@@ -123,13 +123,22 @@
     own_scaled = scale * element
     rows = [jnp.sum(r_col * m, axis=0, keepdims=True) for m in [element] + faces]
     rows.append(r_row * jnp.sum(on_diagonal, axis=0, keepdims=True) / damping)
-    stacked = jnp.concatenate(
-        [own_scaled, scaled[4], scaled[5]] + rows + [jnp.zeros((8, NP), f32)], axis=0)
-    high, low = halves(stacked)
-    own_w[:, 0:64] = high
-    own_w[:, 64:128] = high
-    own_w[:, 128:192] = low
-    own_w[:, 192:256] = low
+
+    def lay(weights, matrix):
+        high, low = halves(matrix)
+        weights[:, 0:64] = high
+        weights[:, 64:128] = high
+        weights[:, 128:192] = low
+        weights[:, 192:256] = low
+
+    lay(own_w, jnp.concatenate([own_scaled, scaled[4], scaled[5]], axis=0))
+
+    reduce_rows = jnp.concatenate(rows[0:7] + [jnp.zeros((1, NP), f32)], axis=0)
+    scaled_rows = reduce_rows * (damping / jnp.sum(on_diagonal, axis=0, keepdims=True))
+    products = [jnp.dot(scaled_rows, m, precision=highest, preferred_element_type=f32)
+                for m in [element] + faces]
+    lay(path_w, jnp.concatenate(
+        [2.0 * reduce_rows - products[0]] + products[1:] + [rows[7], jnp.zeros((7, NP), f32)], axis=0))
     for d in range(4):
         high, low = halves(scaled[d])
         side_w[0:64, d * 64:d * 64 + 64] = high
@@ -187,12 +196,26 @@
             src_ref=values.at[s], dst_ref=halo.at[s], send_sem=send.at[s], recv_sem=recv.at[s],
             device_id=target[s], device_id_type=MESH)
 
+    paths = functools.partial(small, qsend, qhalo, qsend_sem, qrecv_sem)
     labels = functools.partial(small, asend, ahalo, asend_sem, arecv_sem)
     scalars = functools.partial(small, tsend, thalo, tsend_sem, trecv_sem)
 
-    for s in range(4):
+    def follow(x, carry):
+        for y in range(SIDE):
+            col, slot = x * SIDE + y, (x + 1) * PADS + y + 1
+            high, low = p1h[slot], p1l[slot]
+            field[col] = jnp.dot(path_w[...], jnp.concatenate([high, low, high, low], axis=0),
+                                 preferred_element_type=f32)
+        return carry
+
+    lax.fori_loop(0, SIDE, follow, 0)
+    for s in range(4):
+        for c in range(SIDE):
+            qsend[s, c] = field[SOURCE[s](c), 8 + 8 * s:16 + 8 * s, :]
+
         @pl.when(sends[s])
         def _(s=s):
+            paths(s).start()
             labels(s).start()
 
     def gather_first(s1, r1, sems, row):
@@ -244,6 +267,7 @@
         @pl.when(jnp.logical_not(has[s]))
         def _(s=s):
             thalo[s] = jnp.zeros((SIDE, EZ), f32)
+            qhalo[s] = jnp.zeros((SIDE, 8, EZ), f32)
             ahalo[s] = jnp.zeros((SIDE, EZ), jnp.int32)
             for c in range(SIDE):
                 slot = padded_slot(s, c)
@@ -259,7 +283,7 @@
         high, low = high_ref[slot], low_ref[slot]
         g = jnp.dot(own_matrix[...], jnp.concatenate([high, low, high, low], axis=0),
                     preferred_element_type=f32)
-        return g[0:64] - after(g[64:128]) - before(g[128:192]), g[192:200]
+        return g[0:64] - after(g[64:128]) - before(g[128:192])
 
     def side_part(high_ref, low_ref, slot):
         around = (slot - PADS, slot + PADS, slot - 1, slot + 1)
@@ -272,14 +296,10 @@
     def second(x, y):
         col, slot = x * SIDE + y, (x + 1) * PADS + y + 1
         before_it = u1[col]
-        own, from_u1 = own_part(p1h, p1l, slot)
-        value = 2.0 * before_it - own + side_part(p1h, p1l, slot)
+        value = 2.0 * before_it - own_part(p1h, p1l, slot) + side_part(p1h, p1l, slot)
         u2[col] = value
         p2h[slot], p2l[slot] = halves(value)
-        own, from_u2 = own_part(p2h, p2l, slot)
-        base_ref[col] = value + before_it - own
-        total = from_u1[7:8] - from_u2[0:1] + after(from_u2[5:6]) + before(from_u2[6:7])
-        trow[col] = jnp.where(iota((8, EZ), 0) == 0, total, from_u2)
+        base_ref[col] = value + before_it - own_part(p2h, p2l, slot)
 
     def arrive(make, halo, high_ref, low_ref, s, c):
         @pl.when(has[s])
@@ -297,6 +317,29 @@
         return carry
 
     lax.fori_loop(0, 2, interior, 0)
+
+    for s in range(4):
+        @pl.when(has[s])
+        def _(s=s):
+            paths(s).wait_recv()
+    for x in range(SIDE):
+        for y in range(SIDE):
+            col = x * SIDE + y
+            value = field[col, 0:8, :] + after(field[col, 40:48, :]) + before(field[col, 48:56, :])
+            value += field[col - SIDE, 8:16, :] if x > 0 else qhalo[0, y]
+            value += field[col + SIDE, 16:24, :] if x < SIDE - 1 else qhalo[1, y]
+            value += field[col - 1, 24:32, :] if y > 0 else qhalo[2, x]
+            value += field[col + 1, 32:40, :] if y < SIDE - 1 else qhalo[3, x]
+            total = field[col, 56:57, :] - value[0:1] + after(value[5:6]) + before(value[6:7])
+            trow[col] = jnp.where(iota((8, EZ), 0) == 0, total, value)
+    for s in range(4):
+        for c in range(SIDE):
+            tsend[s, c:c + 1, :] = trow[SOURCE[s](c), s + 1:s + 2, :]
+
+        @pl.when(sends[s])
+        def _(s=s):
+            scalars(s).start()
+
     for c in range(SIDE):
         for s in (2, 3):
             arrive1(s, c)
@@ -311,36 +354,6 @@
     for c in (1, 2):
         for s in (2, 3):
             start(face2, s, c)
-    for c in range(SIDE):
-        arrive1(0, c)
-        arrive1(1, c)
-        second(0, c)
-        second(SIDE - 1, c)
-        start(face2, 0, c)
-        start(face2, 1, c)
-        if c in (0, SIDE - 1):
-            s = 3 if c == 0 else 2
-            start(face2, s, 0)
-            start(face2, s, SIDE - 1)
-
-    for s in range(4):
-        for c in range(SIDE):
-            tsend[s, c:c + 1, :] = trow[SOURCE[s](c), s + 1:s + 2, :]
-
-        @pl.when(sends[s])
-        def _(s=s):
-            scalars(s).start()
-
-    def last(x, y):
-        col, slot = x * SIDE + y, (x + 1) * PADS + y + 1
-        base_ref[col] += side_part(p2h, p2l, slot)
-
-    def last_interior(i, carry):
-        last(1, i + 1)
-        last(2, i + 1)
-        return carry
-
-    lax.fori_loop(0, 2, last_interior, 0)
 
     for s in range(4):
         @pl.when(has[s])
@@ -365,6 +378,31 @@
     gather_first(s1b, r1b, gsem_b, jnp.where(in_group, sums[0:1], 0.0))
 
     for c in range(SIDE):
+        arrive1(0, c)
+        arrive1(1, c)
+        second(0, c)
+        second(SIDE - 1, c)
+        start(face2, 0, c)
+        start(face2, 1, c)
+        if c in (0, SIDE - 1):
+            s = 3 if c == 0 else 2
+            start(face2, s, 0)
+            start(face2, s, SIDE - 1)
+
+    gather_second(r1b, s2b, r2b, gsem_b)
+
+    def last(x, y):
+        col, slot = x * SIDE + y, (x + 1) * PADS + y + 1
+        base_ref[col] += side_part(p2h, p2l, slot)
+
+    def last_interior(i, carry):
+        last(1, i + 1)
+        last(2, i + 1)
+        return carry
+
+    lax.fori_loop(0, 2, last_interior, 0)
+
+    for c in range(SIDE):
         for s in (2, 3):
             arrive2(s, c)
 
@@ -374,7 +412,6 @@
         return carry
 
     lax.fori_loop(0, 2, last_y, 0)
-    gather_second(r1b, s2b, r2b, gsem_b)
 
     gains = [jnp.sum(m * p_row, axis=1, keepdims=True) for m in scaled]
     own_gain = p_col - jnp.sum(own_scaled * p_row, axis=1, keepdims=True)
@@ -420,6 +457,7 @@
         def _(s=s):
             labels(s).wait_send()
             scalars(s).wait_send()
+            paths(s).wait_send()
             for c in range(SIDE):
                 face1(s, c).wait_send()
                 face2(s, c).wait_send()
@@ -508,6 +546,7 @@
         pltpu.VMEM((8, 128), f32),
         pltpu.VMEM((zn, 8, 128), f32),
     ]
+    side_groups = pltpu.VMEM((4, SIDE, 8, EZ), f32)
     side_rows = pltpu.VMEM((4, SIDE, EZ), f32)
     side_labels = pltpu.VMEM((4, SIDE, EZ), jnp.int32)
     base, coef, grhs, gpiv, labels = pl.pallas_call(
@@ -526,11 +565,12 @@
             pltpu.VMEM((NP, NP), f32), pltpu.VMEM((6, NP, NP), f32), pltpu.VMEM((NP,), f32),
             pltpu.VMEM((NP,), f32), pltpu.VMEM((1, 1, KC), f32),
             field, field, field, halo, halo, parts, parts, parts, parts,
-            pltpu.VMEM((208, 256), bf16), pltpu.VMEM((128, 256), bf16),
+            pltpu.VMEM((192, 256), bf16), pltpu.VMEM((128, 256), bf16), pltpu.VMEM((64, 256), bf16),
+            field, side_groups, side_groups,
             pltpu.VMEM((COLS, 8, EZ), f32), side_rows, side_rows, side_labels, side_labels,
             *gather, *gather,
             dma((7,)), dma((SIDE,)), dma((4, SIDE)), dma((4, SIDE)), dma((4, SIDE)), dma((4, SIDE)),
-            dma((4,)), dma((4,)), dma((4,)), dma((4,)), dma((4,)), dma((4,)),
+            dma((4,)), dma((4,)), dma((4,)), dma((4,)), dma((4,)), dma((4,)), dma((4,)), dma((4,)),
         ],
         compiler_params=pltpu.CompilerParams(
             collective_id=0, has_side_effects=True, vmem_limit_bytes=40 * 2**20),

time: 44.1 us -> 38.8 us (0.88); the launches traced: 44 us -> 38.1 us
  Pallas kernels: 43.4 us -> 37.4 us
    pallas_call x1, Pallas kernels: 39.3 us -> 33.4 us  [body(): pl.pallas_call(functools.partial(exchange_kernel, gxn, gyn, zn), out_shap...]
where the time goes in v3:
time: 38.8 us; the launch traced here: 38.1 us
  Pallas kernels  37.4 us (96%)
  between operations  0.64 us (2%)
    pallas_call x1, Pallas kernels, body(): pl.pallas_call(functools.partial(exchange_kernel, gxn, gyn, zn), out_shap...  33.4 us
    pallas_call x1, Pallas kernels, body(): pl.pallas_call(functools.partial(finish_kernel, gxn, gyn, zn), out_shape=...  4.08 us

profile of v3, /device:TPU:1, one launch (start us, length us, event | category | flops | bytes accessed | tf_op | source)
XLA Modules:
  0.0 38.1 jit_solution(6894951868912520267)
XLA Ops:
  0.6 33.4 %exchange.1 = (f32[16,64,256]{2,1,0:T(8,128)S(1)}, bf16[16,64,256]{2,1,0:T(8,128)(2,1)S(1)}, f32[8,8,128]{2,1,0:T(8,128)S(1)}, f32[8,8,128]{2,1,0:T(8,128)S(1)}, s32[32,256]{1,0:T(8,128)S(1)}) custom-call(f32[4,4,64,256]{3,2,1,0:T(8,128)} %rhs_hbm.1, f32[4,4,256]{2,1,0:T(4,128)} %w_hbm.1, s32[4,4,256]{2,1,0:T(4,128)} %agg_hbm.1, f32[64,64]{1,0:T(8,128)} %e_hbm.1, ...), custom_call_target="tpu_custom_call" | custom-call | tf_op jit(solution)/shard_map/exchange/pallas_call | solution.py:552
  34.0 4.1 %finish.1 = (f32[4,4,64,256]{3,2,1,0:T(8,128)}, f32[1,1,32]{2,1,0:T(1,128)}) custom-call(f32[16,64,256]{2,1,0:T(8,128)S(1)} %get-tuple-element.7.base_ref, bf16[16,64,256]{2,1,0:T(8,128)(2,1)S(1)} %get-tuple-element.8.coef_ref, f32[8,8,128]{2,1,0:T(8,128)S(1)} %get-tuple-element.9.grhs_ref, f32[8,8,128]{2,1,0:T(8,128)S(1)} %get-tuple-element.10.gpiv_ref, ...), custom_call_target="tpu_custom_call" | custom-call | tf_op jit(solution)/shard_map/finish/pallas_call | solution.py:581

commit v4 on v3

--- a/solution.py
+++ b/solution.py
@@ -58,7 +58,7 @@
     field, qsend, qhalo, trow, tsend, thalo, asend, ahalo,
     s1a, r1a, s2a, r2a, s1b, r1b, s2b, r2b,
     small_sem, load_sem, send1, recv1, send2, recv2, tsend_sem, trecv_sem, asend_sem, arecv_sem,
-    gsem_a, gsem_b, qsend_sem, qrecv_sem,
+    gsem_a, gsem_b, qsend_sem, qrecv_sem, all_in,
 ):
     gx, gy = lax.axis_index("gx"), lax.axis_index("gy")
     xg, zg = gx // zn, gx % zn
@@ -170,36 +170,6 @@
     def spread(row):
         return jnp.where(in_group, jnp.concatenate([row] * 4, axis=1), 0.0)
 
-    expected = group - 1 + zn - 1 + has[0].astype(jnp.int32) + has[1].astype(jnp.int32)
-    pl.semaphore_wait(barrier, expected)
-
-    def face(values, halo, send, recv, s, c):
-        return pltpu.make_async_remote_copy(
-            src_ref=values.at[SOURCE[s](c)], dst_ref=halo.at[s, c],
-            send_sem=send.at[s, c], recv_sem=recv.at[s, c],
-            device_id=target[s], device_id_type=MESH)
-
-    face1 = functools.partial(face, u1, hal1, send1, recv1)
-    face2 = functools.partial(face, u2, hal2, send2, recv2)
-
-    def start(make, s, c):
-        @pl.when(sends[s])
-        def _():
-            make(s, c).start()
-
-    for c in range(SIDE):
-        for s in range(4):
-            start(face1, s, c)
-
-    def small(values, halo, send, recv, s):
-        return pltpu.make_async_remote_copy(
-            src_ref=values.at[s], dst_ref=halo.at[s], send_sem=send.at[s], recv_sem=recv.at[s],
-            device_id=target[s], device_id_type=MESH)
-
-    paths = functools.partial(small, qsend, qhalo, qsend_sem, qrecv_sem)
-    labels = functools.partial(small, asend, ahalo, asend_sem, arecv_sem)
-    scalars = functools.partial(small, tsend, thalo, tsend_sem, trecv_sem)
-
     def follow(x, carry):
         for y in range(SIDE):
             col, slot = x * SIDE + y, (x + 1) * PADS + y + 1
@@ -213,10 +183,39 @@
         for c in range(SIDE):
             qsend[s, c] = field[SOURCE[s](c), 8 + 8 * s:16 + 8 * s, :]
 
+    expected = group - 1 + zn - 1 + has[0].astype(jnp.int32) + has[1].astype(jnp.int32)
+    pl.semaphore_wait(barrier, expected)
+
+    def face(values, halo, send, recv, s, c):
+        return pltpu.make_async_remote_copy(
+            src_ref=values.at[SOURCE[s](c)], dst_ref=halo.at[s, c],
+            send_sem=send.at[s, c], recv_sem=recv.at[s, c],
+            device_id=target[s], device_id_type=MESH)
+
+    face1 = functools.partial(face, u1, hal1, send1, recv1)
+    face2 = functools.partial(face, u2, hal2, send2, recv2)
+
+    def start(make, s, c):
         @pl.when(sends[s])
+        def _():
+            make(s, c).start()
+
+    def small(values, halo, send, recv, s):
+        return pltpu.make_async_remote_copy(
+            src_ref=values.at[s], dst_ref=halo.at[s], send_sem=send.at[s], recv_sem=recv.at[s],
+            device_id=target[s], device_id_type=MESH)
+
+    paths = functools.partial(small, qsend, qhalo, qsend_sem, qrecv_sem)
+    labels = functools.partial(small, asend, ahalo, asend_sem, arecv_sem)
+    scalars = functools.partial(small, tsend, thalo, tsend_sem, trecv_sem)
+
+    for s in range(4):
+        @pl.when(sends[s])
         def _(s=s):
             paths(s).start()
-            labels(s).start()
+    for c in range(SIDE):
+        for s in (0, 1, 2, 3) if c < 2 else (2, 3):
+            start(face1, s, c)
 
     def gather_first(s1, r1, sems, row):
         s1[...] = row
@@ -259,6 +258,64 @@
         out[...] = r2[...]
         wait_bytes(r1, group - 1, sems.at[0])
         wait_bytes(r2, zn - 1, sems.at[2])
+
+    def pass_on(j, carry):
+        @pl.when(j != zg)
+        def _():
+            pl.semaphore_signal(
+                all_in, inc=1, device_id=(xg * zn + j, gy), device_id_type=MESH)
+        return carry
+
+    lax.fori_loop(0, zn, pass_on, 0)
+    core, yg, yn = gy % 2, gy // 2, gyn // 2
+    chips = gxn * yn
+
+    def far_first(size):
+        half = size // 2
+        return [half - (k + 1) // 2 if k % 2 else half + k // 2 for k in range(size)]
+
+    def direct_first(s1, r1, sems, row):
+        s1[...] = row
+        r1[gx * yn + yg] = row
+        pl.semaphore_wait(all_in, zn - 1)
+
+        def send(dx, dy, to_z):
+            to_x = (xg + dx) % xn * zn + to_z
+            pltpu.make_async_remote_copy(
+                src_ref=s1, dst_ref=r1.at[gx * yn + yg], send_sem=sems.at[0], recv_sem=sems.at[1],
+                device_id=(to_x, (yg + dy) % yn * 2 + core), device_id_type=MESH).start()
+
+        offsets = [(dx, dy) for dx in far_first(xn) for dy in far_first(yn)]
+
+        def step(k, carry):
+            to_z = (zg + jnp.where(k % 2 == 1, zn // 2 - (k + 1) // 2, zn // 2 + k // 2)) % zn
+            for dx, dy in offsets:
+                send(dx, dy, to_z)
+            return carry
+
+        lax.fori_loop(0, zn - 1, step, 0)
+        for dx, dy in offsets[:-1]:
+            send(dx, dy, zg)
+
+    def pair(s2, r2, sems):
+        return pltpu.make_async_remote_copy(
+            src_ref=s2, dst_ref=r2, send_sem=sems.at[2], recv_sem=sems.at[3],
+            device_id=(gx, gy + 1 - 2 * core), device_id_type=MESH)
+
+    def direct_second(r1, s2, r2, sems):
+        wait_bytes(r1, chips - 1, sems.at[1])
+        s2[...] = jnp.zeros_like(s2)
+        for i in range(zn):
+            for y in range(yn):
+                s2[i, pl.ds(2 * y + core, 1), :] = sum(
+                    r1[(q * zn + i) * yn + y] for q in range(xn))
+        pair(s2, r2, sems).start()
+
+    def direct_third(r1, s2, r2, sems, out):
+        pair(s2, r2, sems).wait_recv()
+        out[...] = s2[...] + r2[...]
+        wait_bytes(r1, chips - 1, sems.at[0])
+        pair(s2, r2, sems).wait_send()
 
     gather_first(s1a, r1a, gsem_a, spread(1.0 / (6.0 + shift_ref[0])))
 
@@ -299,7 +356,10 @@
         value = 2.0 * before_it - own_part(p1h, p1l, slot) + side_part(p1h, p1l, slot)
         u2[col] = value
         p2h[slot], p2l[slot] = halves(value)
-        base_ref[col] = value + before_it - own_part(p2h, p2l, slot)
+
+    def second_own(x, y):
+        col, slot = x * SIDE + y, (x + 1) * PADS + y + 1
+        base_ref[col] = u2[col] + u1[col] - own_part(p2h, p2l, slot)
 
     def arrive(make, halo, high_ref, low_ref, s, c):
         @pl.when(has[s])
@@ -314,6 +374,8 @@
     def interior(i, carry):
         second(1, i + 1)
         second(2, i + 1)
+        second_own(1, i + 1)
+        second_own(2, i + 1)
         return carry
 
     lax.fori_loop(0, 2, interior, 0)
@@ -339,6 +401,13 @@
         @pl.when(sends[s])
         def _(s=s):
             scalars(s).start()
+    for c in range(2, SIDE):
+        for s in (0, 1):
+            start(face1, s, c)
+    for s in range(4):
+        @pl.when(sends[s])
+        def _(s=s):
+            labels(s).start()
 
     for c in range(SIDE):
         for s in (2, 3):
@@ -348,6 +417,8 @@
     def side_y(i, carry):
         second(i + 1, 0)
         second(i + 1, SIDE - 1)
+        second_own(i + 1, 0)
+        second_own(i + 1, SIDE - 1)
         return carry
 
     lax.fori_loop(0, 2, side_y, 0)
@@ -375,7 +446,7 @@
     sums = lax.dot_general(
         jnp.ones((8, EZ), f32), jnp.concatenate([total] * 4, axis=0),
         (((1,), (1,)), ((), ())), precision=highest, preferred_element_type=f32)
-    gather_first(s1b, r1b, gsem_b, jnp.where(in_group, sums[0:1], 0.0))
+    direct_first(s1b, r1b, gsem_b, jnp.where(in_group, sums[0:1], 0.0))
 
     for c in range(SIDE):
         arrive1(0, c)
@@ -388,8 +459,10 @@
             s = 3 if c == 0 else 2
             start(face2, s, 0)
             start(face2, s, SIDE - 1)
-
-    gather_second(r1b, s2b, r2b, gsem_b)
+        second_own(0, c)
+        second_own(SIDE - 1, c)
+
+    direct_second(r1b, s2b, r2b, gsem_b)
 
     def last(x, y):
         col, slot = x * SIDE + y, (x + 1) * PADS + y + 1
@@ -450,7 +523,7 @@
     for s in range(4):
         labels_ref[COLS + s * SIDE:COLS + (s + 1) * SIDE, :] = ahalo[s]
     gather_third(r1a, r2a, gsem_a, gpiv_ref)
-    gather_third(r1b, r2b, gsem_b, grhs_ref)
+    direct_third(r1b, s2b, r2b, gsem_b, grhs_ref)
 
     for s in range(4):
         @pl.when(sends[s])
@@ -544,6 +617,12 @@
         pltpu.VMEM((1, 128), f32),
         pltpu.VMEM((group, 1, 128), f32),
         pltpu.VMEM((8, 128), f32),
+        pltpu.VMEM((zn, 8, 128), f32),
+    ]
+    direct = [
+        pltpu.VMEM((1, 128), f32),
+        pltpu.VMEM((gxn * gyn // 2, 1, 128), f32),
+        pltpu.VMEM((zn, 8, 128), f32),
         pltpu.VMEM((zn, 8, 128), f32),
     ]
     side_groups = pltpu.VMEM((4, SIDE, 8, EZ), f32)
@@ -568,9 +647,9 @@
             pltpu.VMEM((192, 256), bf16), pltpu.VMEM((128, 256), bf16), pltpu.VMEM((64, 256), bf16),
             field, side_groups, side_groups,
             pltpu.VMEM((COLS, 8, EZ), f32), side_rows, side_rows, side_labels, side_labels,
-            *gather, *gather,
+            *gather, *direct,
             dma((7,)), dma((SIDE,)), dma((4, SIDE)), dma((4, SIDE)), dma((4, SIDE)), dma((4, SIDE)),
-            dma((4,)), dma((4,)), dma((4,)), dma((4,)), dma((4,)), dma((4,)), dma((4,)), dma((4,)),
+            *[dma((4,))] * 8, pltpu.SemaphoreType.REGULAR,
         ],
         compiler_params=pltpu.CompilerParams(
             collective_id=0, has_side_effects=True, vmem_limit_bytes=40 * 2**20),

time: 38.8 us -> 33.9 us (0.87); the launches traced: 38.1 us -> 33.8 us
  Pallas kernels: 37.4 us -> 33.2 us
    pallas_call x1, Pallas kernels: 33.4 us -> 29.1 us  [body(): pl.pallas_call(functools.partial(exchange_kernel, gxn, gyn, zn), out_shap...]
where the time goes in v4:
time: 33.9 us; the launch traced here: 33.8 us
  Pallas kernels  33.2 us (98%)
  between operations  0.64 us (2%)
    pallas_call x1, Pallas kernels, body(): pl.pallas_call(functools.partial(exchange_kernel, gxn, gyn, zn), out_shap...  29.1 us
    pallas_call x1, Pallas kernels, body(): pl.pallas_call(functools.partial(finish_kernel, gxn, gyn, zn), out_shape=...  4.08 us

profile of v4, /device:TPU:1, one launch (start us, length us, event | category | flops | bytes accessed | tf_op | source)
XLA Modules:
  0.0 33.8 jit_solution(5444430256037271024)
XLA Ops:
  0.6 29.1 %exchange.1 = (f32[16,64,256]{2,1,0:T(8,128)S(1)}, bf16[16,64,256]{2,1,0:T(8,128)(2,1)S(1)}, f32[8,8,128]{2,1,0:T(8,128)S(1)}, f32[8,8,128]{2,1,0:T(8,128)S(1)}, s32[32,256]{1,0:T(8,128)S(1)}) custom-call(f32[4,4,64,256]{3,2,1,0:T(8,128)} %rhs_hbm.1, f32[4,4,256]{2,1,0:T(4,128)} %w_hbm.1, s32[4,4,256]{2,1,0:T(4,128)} %agg_hbm.1, f32[64,64]{1,0:T(8,128)} %e_hbm.1, ...), custom_call_target="tpu_custom_call" | custom-call | tf_op jit(solution)/shard_map/exchange/pallas_call | solution.py:631
  29.7 4.1 %finish.1 = (f32[4,4,64,256]{3,2,1,0:T(8,128)}, f32[1,1,32]{2,1,0:T(1,128)}) custom-call(f32[16,64,256]{2,1,0:T(8,128)S(1)} %get-tuple-element.7.base_ref, bf16[16,64,256]{2,1,0:T(8,128)(2,1)S(1)} %get-tuple-element.8.coef_ref, f32[8,8,128]{2,1,0:T(8,128)S(1)} %get-tuple-element.9.grhs_ref, f32[8,8,128]{2,1,0:T(8,128)S(1)} %get-tuple-element.10.gpiv_ref, ...), custom_call_target="tpu_custom_call" | custom-call | tf_op jit(solution)/shard_map/finish/pallas_call | solution.py:660

commit v5 on v4

--- a/solution.py
+++ b/solution.py
@@ -55,10 +55,10 @@
     rhs_hbm, w_hbm, agg_hbm, e_hbm, f_hbm, r_hbm, p_hbm, shift_hbm,
     base_ref, coef_ref, grhs_ref, gpiv_ref, labels_ref,
     w_ref, agg_ref, e_ref, f_ref, r_ref, p_ref, shift_ref, rhs_v, u1, u2, hal1, hal2, p1h, p1l, p2h, p2l, own_w, side_w, path_w,
-    field, qsend, qhalo, trow, tsend, thalo, asend, ahalo,
+    field, qsend, qhalo, trow, asend, ahalo, placed, sib_out, sib_in,
     s1a, r1a, s2a, r2a, s1b, r1b, s2b, r2b,
-    small_sem, load_sem, send1, recv1, send2, recv2, tsend_sem, trecv_sem, asend_sem, arecv_sem,
-    gsem_a, gsem_b, qsend_sem, qrecv_sem, all_in,
+    small_sem, load_sem, send1, recv1, send2, recv2, asend_sem, arecv_sem,
+    gsem_a, gsem_b, qsend_sem, qrecv_sem, sib_sem, all_in,
 ):
     gx, gy = lax.axis_index("gx"), lax.axis_index("gy")
     xg, zg = gx // zn, gx % zn
@@ -158,12 +158,13 @@
         lax.fori_loop(0, SIDE, first, 0)
 
     for x in range(SIDE):
-        labels_ref[x * SIDE:(x + 1) * SIDE, :] = agg_ref[x]
-    asend[0] = agg_ref[SIDE - 1]
-    asend[1] = agg_ref[0]
-    for c in range(SIDE):
-        asend[2, c:c + 1, :] = agg_ref[c, SIDE - 1:SIDE, :]
-        asend[3, c:c + 1, :] = agg_ref[c, 0:1, :]
+        labels_ref[x * SIDE:(x + 1) * SIDE, :] = agg_ref[x].astype(f32)
+    for s in range(4):
+        for c in range(SIDE):
+            x, y = SOURCE[s](c) // SIDE, SOURCE[s](c) % SIDE
+            asend[s, c:c + 1, :] = w_ref[x, y:y + 1, :]
+            asend[s, SIDE + c:SIDE + c + 1, :] = agg_ref[x, y:y + 1, :].astype(f32)
+    placed[...] = jnp.zeros_like(placed)
 
     in_group = iota((1, 128), 1) // KC == xg
 
@@ -207,14 +208,14 @@
 
     paths = functools.partial(small, qsend, qhalo, qsend_sem, qrecv_sem)
     labels = functools.partial(small, asend, ahalo, asend_sem, arecv_sem)
-    scalars = functools.partial(small, tsend, thalo, tsend_sem, trecv_sem)
 
     for s in range(4):
         @pl.when(sends[s])
         def _(s=s):
             paths(s).start()
+            labels(s).start()
     for c in range(SIDE):
-        for s in (0, 1, 2, 3) if c < 2 else (2, 3):
+        for s in (0, 1, 2, 3) if c < SIDE - 1 else (2, 3):
             start(face1, s, c)
 
     def gather_first(s1, r1, sems, row):
@@ -274,15 +275,16 @@
         half = size // 2
         return [half - (k + 1) // 2 if k % 2 else half + k // 2 for k in range(size)]
 
-    def direct_first(s1, r1, sems, row):
-        s1[...] = row
-        r1[gx * yn + yg] = row
+    def direct_first(rows):
+        s1b[...] = rows
+        r1b[gx * yn + yg] = rows
         pl.semaphore_wait(all_in, zn - 1)
 
         def send(dx, dy, to_z):
             to_x = (xg + dx) % xn * zn + to_z
             pltpu.make_async_remote_copy(
-                src_ref=s1, dst_ref=r1.at[gx * yn + yg], send_sem=sems.at[0], recv_sem=sems.at[1],
+                src_ref=s1b, dst_ref=r1b.at[gx * yn + yg], send_sem=gsem_b.at[0],
+                recv_sem=gsem_b.at[1],
                 device_id=(to_x, (yg + dy) % yn * 2 + core), device_id_type=MESH).start()
 
         offsets = [(dx, dy) for dx in far_first(xn) for dy in far_first(yn)]
@@ -297,25 +299,50 @@
         for dx, dy in offsets[:-1]:
             send(dx, dy, zg)
 
-    def pair(s2, r2, sems):
-        return pltpu.make_async_remote_copy(
-            src_ref=s2, dst_ref=r2, send_sem=sems.at[2], recv_sem=sems.at[3],
-            device_id=(gx, gy + 1 - 2 * core), device_id_type=MESH)
-
-    def direct_second(r1, s2, r2, sems):
-        wait_bytes(r1, chips - 1, sems.at[1])
-        s2[...] = jnp.zeros_like(s2)
+    pair = pltpu.make_async_remote_copy(
+        src_ref=s2b, dst_ref=r2b, send_sem=gsem_b.at[2], recv_sem=gsem_b.at[3],
+        device_id=(gx, gy + 1 - 2 * core), device_id_type=MESH)
+
+    def direct_second():
+        wait_bytes(r1b, chips - 1, gsem_b.at[1])
+        for q in range(xn):
+            for i in range(zn):
+                for y in range(yn):
+                    at = (q * zn + i) * yn + y
+                    placed[q, i, pl.ds(2 * y + core, 1), :] = r1b[at]
+        kind, sub = iota((8, 128), 1) // KC, iota((8, 128), 0)
+        zero = jnp.zeros((8, 128), f32)
+        step_y, edge = jnp.where(core == 1, 1, 7), jnp.where(core == 1, 0, 7)
+
+        def source(q, i):
+            return placed[q, i] if q < xn else zero
+
         for i in range(zn):
-            for y in range(yn):
-                s2[i, pl.ds(2 * y + core, 1), :] = sum(
-                    r1[(q * zn + i) * yn + y] for q in range(xn))
-        pair(s2, r2, sems).start()
-
-    def direct_third(r1, s2, r2, sems, out):
-        pair(s2, r2, sems).wait_recv()
-        out[...] = s2[...] + r2[...]
-        wait_bytes(r1, chips - 1, sems.at[0])
-        pair(s2, r2, sems).wait_send()
+            total = zero
+            for r in range(4):
+                own = source(r, i)
+                if i > 0:
+                    left = source((1 + r) % 4, i - 1)
+                else:
+                    left = source(r, zn - 1) if r < 3 else zero
+                if i < zn - 1:
+                    right = source((2 + r) % 4, i + 1)
+                else:
+                    right = source((3 + r) % 4, 0) if (3 + r) % 4 else zero
+                beside = jnp.where(
+                    sub == edge, 0.0, pltpu.roll(source((3 + r) % 4, i), step_y, 0))
+                moved = jnp.where(kind < 2, jnp.where(kind == 0, own, left),
+                                  jnp.where(kind == 2, right, beside))
+                total += pltpu.roll(moved, KC * r, 1) if r else moved
+            s2b[i] = total
+        pair.start()
+
+    def direct_third(out):
+        pair.wait_recv()
+        out[...] = s2b[...] + r2b[...]
+        wait_bytes(r1b, chips - 1, gsem_b.at[0])
+        pair.wait_send()
+        sib_copy.wait_send()
 
     gather_first(s1a, r1a, gsem_a, spread(1.0 / (6.0 + shift_ref[0])))
 
@@ -323,9 +350,8 @@
     for s in range(4):
         @pl.when(jnp.logical_not(has[s]))
         def _(s=s):
-            thalo[s] = jnp.zeros((SIDE, EZ), f32)
             qhalo[s] = jnp.zeros((SIDE, 8, EZ), f32)
-            ahalo[s] = jnp.zeros((SIDE, EZ), jnp.int32)
+            ahalo[s] = jnp.zeros((2 * SIDE, EZ), f32)
             for c in range(SIDE):
                 slot = padded_slot(s, c)
                 p1h[slot] = nothing
@@ -384,6 +410,7 @@
         @pl.when(has[s])
         def _(s=s):
             paths(s).wait_recv()
+            labels(s).wait_recv()
     for x in range(SIDE):
         for y in range(SIDE):
             col = x * SIDE + y
@@ -394,20 +421,52 @@
             value += field[col + 1, 32:40, :] if y < SIDE - 1 else qhalo[3, x]
             total = field[col, 56:57, :] - value[0:1] + after(value[5:6]) + before(value[6:7])
             trow[col] = jnp.where(iota((8, EZ), 0) == 0, total, value)
+
     for s in range(4):
+        labels_ref[COLS + s * SIDE:COLS + (s + 1) * SIDE, :] = ahalo[s, SIDE:2 * SIDE, :]
+    levels = iota((KC, EZ), 0)
+    float_levels = levels.astype(f32)
+
+    def to_side(s):
+        total = jnp.zeros((KC, EZ), f32)
+        side = s + 1 - 2 * (s % 2)
         for c in range(SIDE):
-            tsend[s, c:c + 1, :] = trow[SOURCE[s](c), s + 1:s + 2, :]
-
-        @pl.when(sends[s])
-        def _(s=s):
-            scalars(s).start()
-    for c in range(2, SIDE):
-        for s in (0, 1):
-            start(face1, s, c)
-    for s in range(4):
-        @pl.when(sends[s])
-        def _(s=s):
-            labels(s).start()
+            row = trow[SOURCE[s](c), s + 1:s + 2, :] * ahalo[side, c:c + 1, :]
+            total += jnp.where(ahalo[side, SIDE + c:SIDE + c + 1, :] == float_levels, row, 0.0)
+        return total
+
+    up, down = to_side(2), to_side(3)
+    sib_out[...] = jnp.where(core == 0, up, down)
+    sib_copy = pltpu.make_async_remote_copy(
+        src_ref=sib_out, dst_ref=sib_in, send_sem=sib_sem.at[0], recv_sem=sib_sem.at[1],
+        device_id=(gx, gy + 1 - 2 * core), device_id_type=MESH)
+    sib_copy.start()
+    total = jnp.zeros((KC, EZ), f32)
+    for x in range(SIDE):
+        for y in range(SIDE):
+            col = x * SIDE + y
+            row = trow[col, 0:1, :]
+            if x > 0:
+                row += trow[col - SIDE, 1:2, :]
+            if x < SIDE - 1:
+                row += trow[col + SIDE, 2:3, :]
+            if y > 0:
+                row += trow[col - 1, 3:4, :]
+            if y < SIDE - 1:
+                row += trow[col + 1, 4:5, :]
+            row = row * w_ref[x, y:y + 1, :]
+            total += jnp.where(agg_ref[x, y:y + 1, :] == levels, row, 0.0)
+    to_x = [to_side(0), to_side(1)]
+    sib_copy.wait_recv()
+    parts = jnp.concatenate([total + sib_in[...]] + to_x + [jnp.where(core == 0, down, up)], axis=0)
+    high = parts.astype(bf16)
+    middle, low = halves(parts - high.astype(f32))
+    sums = lax.dot_general(
+        jnp.ones((16, 3 * EZ), bf16), jnp.concatenate([high, middle, low], axis=1),
+        (((1,), (1,)), ((), ())), preferred_element_type=f32)
+    direct_first(sums[0:1])
+    for s in (0, 1):
+        start(face1, s, SIDE - 1)
 
     for c in range(SIDE):
         for s in (2, 3):
@@ -425,28 +484,6 @@
     for c in (1, 2):
         for s in (2, 3):
             start(face2, s, c)
-
-    for s in range(4):
-        @pl.when(has[s])
-        def _(s=s):
-            scalars(s).wait_recv()
-
-    levels = iota((KC, EZ), 0)
-    total = jnp.zeros((KC, EZ), f32)
-    for x in range(SIDE):
-        for y in range(SIDE):
-            col = x * SIDE + y
-            row = trow[col, 0:1, :]
-            row += trow[col - SIDE, 1:2, :] if x > 0 else thalo[0, y:y + 1, :]
-            row += trow[col + SIDE, 2:3, :] if x < SIDE - 1 else thalo[1, y:y + 1, :]
-            row += trow[col - 1, 3:4, :] if y > 0 else thalo[2, x:x + 1, :]
-            row += trow[col + 1, 4:5, :] if y < SIDE - 1 else thalo[3, x:x + 1, :]
-            row = row * w_ref[x, y:y + 1, :]
-            total += jnp.where(agg_ref[x, y:y + 1, :] == levels, row, 0.0)
-    sums = lax.dot_general(
-        jnp.ones((8, EZ), f32), jnp.concatenate([total] * 4, axis=0),
-        (((1,), (1,)), ((), ())), precision=highest, preferred_element_type=f32)
-    direct_first(s1b, r1b, gsem_b, jnp.where(in_group, sums[0:1], 0.0))
 
     for c in range(SIDE):
         arrive1(0, c)
@@ -462,7 +499,6 @@
         second_own(0, c)
         second_own(SIDE - 1, c)
 
-    direct_second(r1b, s2b, r2b, gsem_b)
 
     def last(x, y):
         col, slot = x * SIDE + y, (x + 1) * PADS + y + 1
@@ -509,6 +545,7 @@
         return carry
 
     lax.fori_loop(0, COLS, coefficients, 0)
+    direct_second()
 
     for c in range(SIDE):
         arrive2(0, c)
@@ -516,20 +553,13 @@
         last(0, c)
         last(SIDE - 1, c)
 
-    for s in range(4):
-        @pl.when(has[s])
-        def _(s=s):
-            labels(s).wait_recv()
-    for s in range(4):
-        labels_ref[COLS + s * SIDE:COLS + (s + 1) * SIDE, :] = ahalo[s]
     gather_third(r1a, r2a, gsem_a, gpiv_ref)
-    direct_third(r1b, s2b, r2b, gsem_b, grhs_ref)
+    direct_third(grhs_ref)
 
     for s in range(4):
         @pl.when(sends[s])
         def _(s=s):
             labels(s).wait_send()
-            scalars(s).wait_send()
             paths(s).wait_send()
             for c in range(SIDE):
                 face1(s, c).wait_send()
@@ -549,7 +579,7 @@
     rhs = [grhs_ref[i] for i in range(zn)]
     pivot = [gpiv_ref[i] for i in range(zn)]
 
-    def sweep(repeat, now):
+    def sweep(now):
         new = []
         wrap_low = jnp.where(lane < KC, 0.0, pltpu.roll(now[zn - 1], KC, 1))
         wrap_high = jnp.where(lane >= 128 - KC, 0.0, pltpu.roll(now[0], 128 - KC, 1))
@@ -564,7 +594,9 @@
             new.append(total * pivot[i])
         return tuple(new)
 
-    now = lax.fori_loop(0, ITC - 1, sweep, tuple(a * b for a, b in zip(rhs, pivot)))
+    now = tuple(a * b for a, b in zip(rhs, pivot))
+    for repeat in range(ITC - 1):
+        now = sweep(now)
     for i in range(zn):
         coarse[i] = now[i]
 
@@ -583,7 +615,7 @@
         jnp.where(sub < 4, sides[0], sides[1]), jnp.where(sub < 4, sides[2], sides[3])]
     for i in range(4):
         for half in range(2):
-            picked = labels[i * 8:i * 8 + 8, half * 128:half * 128 + 128]
+            picked = labels[i * 8:i * 8 + 8, half * 128:half * 128 + 128].astype(jnp.int32)
             lifted[i * 8:i * 8 + 8, half * 128:half * 128 + 128] = jnp.take_along_axis(
                 tables[i], picked, axis=1)
     lifted[32:48, :] = after(lifted[0:16, :])
@@ -626,8 +658,9 @@
         pltpu.VMEM((zn, 8, 128), f32),
     ]
     side_groups = pltpu.VMEM((4, SIDE, 8, EZ), f32)
-    side_rows = pltpu.VMEM((4, SIDE, EZ), f32)
-    side_labels = pltpu.VMEM((4, SIDE, EZ), jnp.int32)
+    side_rows = pltpu.VMEM((4, 2 * SIDE, EZ), f32)
+    placed = pltpu.VMEM((gxn // zn, zn, 8, 128), f32)
+    sibling = pltpu.VMEM((KC, EZ), f32)
     base, coef, grhs, gpiv, labels = pl.pallas_call(
         functools.partial(exchange_kernel, gxn, gyn, zn),
         out_shape=(
@@ -635,7 +668,7 @@
             jax.ShapeDtypeStruct((COLS, NP, 256), bf16),
             jax.ShapeDtypeStruct((zn, 8, 128), f32),
             jax.ShapeDtypeStruct((zn, 8, 128), f32),
-            jax.ShapeDtypeStruct((2 * COLS, EZ), jnp.int32),
+            jax.ShapeDtypeStruct((2 * COLS, EZ), f32),
         ),
         in_specs=[pl.BlockSpec(memory_space=pltpu.HBM)] * 8,
         out_specs=(vmem,) * 5,
@@ -646,10 +679,10 @@
             field, field, field, halo, halo, parts, parts, parts, parts,
             pltpu.VMEM((192, 256), bf16), pltpu.VMEM((128, 256), bf16), pltpu.VMEM((64, 256), bf16),
             field, side_groups, side_groups,
-            pltpu.VMEM((COLS, 8, EZ), f32), side_rows, side_rows, side_labels, side_labels,
+            pltpu.VMEM((COLS, 8, EZ), f32), side_rows, side_rows, placed, sibling, sibling,
             *gather, *direct,
             dma((7,)), dma((SIDE,)), dma((4, SIDE)), dma((4, SIDE)), dma((4, SIDE)), dma((4, SIDE)),
-            *[dma((4,))] * 8, pltpu.SemaphoreType.REGULAR,
+            *[dma((4,))] * 6, dma((2,)), pltpu.SemaphoreType.REGULAR,
         ],
         compiler_params=pltpu.CompilerParams(
             collective_id=0, has_side_effects=True, vmem_limit_bytes=40 * 2**20),

time: 33.9 us -> 33.1 us (0.976)
  the two profiles are of different devices: /device:TPU:1 before, /device:TPU:3 now
where the time goes in v5:
time: 33.1 us; the launch traced here: 33 us
  Pallas kernels  32.3 us (98%)
  between operations  0.64 us (2%)
    pallas_call x1, Pallas kernels, body(): pl.pallas_call(functools.partial(exchange_kernel, gxn, gyn, zn), out_shap...  28.4 us
    pallas_call x1, Pallas kernels, body(): pl.pallas_call(functools.partial(finish_kernel, gxn, gyn, zn), out_shape=...  3.97 us

profile of v5, /device:TPU:3, one launch (start us, length us, event | category | flops | bytes accessed | tf_op | source)
XLA Modules:
  0.0 33.0 jit_solution(7001763122497183605)
XLA Ops:
  0.6 28.4 %exchange.1 = (f32[16,64,256]{2,1,0:T(8,128)S(1)}, bf16[16,64,256]{2,1,0:T(8,128)(2,1)S(1)}, f32[8,8,128]{2,1,0:T(8,128)S(1)}, f32[8,8,128]{2,1,0:T(8,128)S(1)}, f32[32,256]{1,0:T(8,128)S(1)}) custom-call(f32[4,4,64,256]{3,2,1,0:T(8,128)} %rhs_hbm.1, f32[4,4,256]{2,1,0:T(4,128)} %w_hbm.1, s32[4,4,256]{2,1,0:T(4,128)} %agg_hbm.1, f32[64,64]{1,0:T(8,128)} %e_hbm.1, ...), custom_call_target="tpu_custom_call" | custom-call | tf_op jit(solution)/shard_map/exchange/pallas_call | solution.py:664
  29.0 4.0 %finish.1 = (f32[4,4,64,256]{3,2,1,0:T(8,128)}, f32[1,1,32]{2,1,0:T(1,128)}) custom-call(f32[16,64,256]{2,1,0:T(8,128)S(1)} %get-tuple-element.7.base_ref, bf16[16,64,256]{2,1,0:T(8,128)(2,1)S(1)} %get-tuple-element.8.coef_ref, f32[8,8,128]{2,1,0:T(8,128)S(1)} %get-tuple-element.9.grhs_ref, f32[8,8,128]{2,1,0:T(8,128)S(1)} %get-tuple-element.10.gpiv_ref, ...), custom_call_target="tpu_custom_call" | custom-call | tf_op jit(solution)/shard_map/finish/pallas_call | solution.py:693

commit v6 on v5

--- a/solution.py
+++ b/solution.py
@@ -15,6 +15,7 @@
 COLS = SIDE * SIDE
 PADS = SIDE + 2
 damping = 0.8
+SPLIT = 3
 highest = lax.Precision.HIGHEST
 MESH = pl.DeviceIdType.MESH
 f32, bf16 = jnp.float32, jnp.bfloat16
@@ -53,7 +54,7 @@
 def exchange_kernel(
     gxn, gyn, zn,
     rhs_hbm, w_hbm, agg_hbm, e_hbm, f_hbm, r_hbm, p_hbm, shift_hbm,
-    base_ref, coef_ref, grhs_ref, gpiv_ref, labels_ref,
+    base_ref, coef_ref, coarse_ref, labels_ref,
     w_ref, agg_ref, e_ref, f_ref, r_ref, p_ref, shift_ref, rhs_v, u1, u2, hal1, hal2, p1h, p1l, p2h, p2l, own_w, side_w, path_w,
     field, qsend, qhalo, trow, asend, ahalo, placed, sib_out, sib_in,
     s1a, r1a, s2a, r2a, s1b, r1b, s2b, r2b,
@@ -253,12 +254,6 @@
             return carry
 
         lax.fori_loop(0, zn, step, 0)
-
-    def gather_third(r1, r2, sems, out):
-        wait_bytes(r2, zn - 1, sems.at[3])
-        out[...] = r2[...]
-        wait_bytes(r1, group - 1, sems.at[0])
-        wait_bytes(r2, zn - 1, sems.at[2])
 
     def pass_on(j, carry):
         @pl.when(j != zg)
@@ -337,12 +332,12 @@
             s2b[i] = total
         pair.start()
 
-    def direct_third(out):
+    def solve_coarse():
+        wait_bytes(r2a, zn - 1, gsem_a.at[3])
         pair.wait_recv()
-        out[...] = s2b[...] + r2b[...]
-        wait_bytes(r1b, chips - 1, gsem_b.at[0])
-        pair.wait_send()
-        sib_copy.wait_send()
+        now = coarse_sweeps([s2b[i] + r2b[i] for i in range(zn)], [r2a[i] for i in range(zn)])
+        for i in range(zn):
+            coarse_ref[i] = now[i]
 
     gather_first(s1a, r1a, gsem_a, spread(1.0 / (6.0 + shift_ref[0])))
 
@@ -548,13 +543,18 @@
     direct_second()
 
     for c in range(SIDE):
+        if c == SPLIT:
+            solve_coarse()
         arrive2(0, c)
         arrive2(1, c)
         last(0, c)
         last(SIDE - 1, c)
 
-    gather_third(r1a, r2a, gsem_a, gpiv_ref)
-    direct_third(grhs_ref)
+    wait_bytes(r1a, group - 1, gsem_a.at[0])
+    wait_bytes(r2a, zn - 1, gsem_a.at[2])
+    wait_bytes(r1b, chips - 1, gsem_b.at[0])
+    pair.wait_send()
+    sib_copy.wait_send()
 
     for s in range(4):
         @pl.when(sends[s])
@@ -566,20 +566,12 @@
                 face2(s, c).wait_send()
 
 
-def finish_kernel(
-    gxn, gyn, zn,
-    base_ref, coef_ref, grhs_ref, gpiv_ref, labels,
-    out_hbm, corr_ref,
-    out_v, coarse, lifted, out_sem,
-):
-    gx, gy = lax.axis_index("gx"), lax.axis_index("gy")
+def coarse_sweeps(rhs, pivot):
+    zn = len(rhs)
     lane, sub = iota((8, 128), 1), iota((8, 128), 0)
     level = lane % KC
 
-    rhs = [grhs_ref[i] for i in range(zn)]
-    pivot = [gpiv_ref[i] for i in range(zn)]
-
-    def sweep(now):
+    def sweep(repeat, now):
         new = []
         wrap_low = jnp.where(lane < KC, 0.0, pltpu.roll(now[zn - 1], KC, 1))
         wrap_high = jnp.where(lane >= 128 - KC, 0.0, pltpu.roll(now[0], 128 - KC, 1))
@@ -594,11 +586,17 @@
             new.append(total * pivot[i])
         return tuple(new)
 
-    now = tuple(a * b for a, b in zip(rhs, pivot))
-    for repeat in range(ITC - 1):
-        now = sweep(now)
-    for i in range(zn):
-        coarse[i] = now[i]
+    return lax.fori_loop(0, ITC - 1, sweep, tuple(a * b for a, b in zip(rhs, pivot)))
+
+
+def finish_kernel(
+    gxn, gyn, zn,
+    base_ref, coef_ref, coarse, labels,
+    out_hbm, corr_ref,
+    out_v, lifted, out_sem,
+):
+    gx, gy = lax.axis_index("gx"), lax.axis_index("gy")
+    lane, sub = iota((8, 128), 1), iota((8, 128), 0)
 
     def table(ax, ay):
         shifted = ax + zn
@@ -661,17 +659,16 @@
     side_rows = pltpu.VMEM((4, 2 * SIDE, EZ), f32)
     placed = pltpu.VMEM((gxn // zn, zn, 8, 128), f32)
     sibling = pltpu.VMEM((KC, EZ), f32)
-    base, coef, grhs, gpiv, labels = pl.pallas_call(
+    base, coef, coarse, labels = pl.pallas_call(
         functools.partial(exchange_kernel, gxn, gyn, zn),
         out_shape=(
             jax.ShapeDtypeStruct((COLS, NP, EZ), f32),
             jax.ShapeDtypeStruct((COLS, NP, 256), bf16),
             jax.ShapeDtypeStruct((zn, 8, 128), f32),
-            jax.ShapeDtypeStruct((zn, 8, 128), f32),
             jax.ShapeDtypeStruct((2 * COLS, EZ), f32),
         ),
         in_specs=[pl.BlockSpec(memory_space=pltpu.HBM)] * 8,
-        out_specs=(vmem,) * 5,
+        out_specs=(vmem,) * 4,
         scratch_shapes=[
             pltpu.VMEM((SIDE, SIDE, EZ), f32), pltpu.VMEM((SIDE, SIDE, EZ), jnp.int32),
             pltpu.VMEM((NP, NP), f32), pltpu.VMEM((6, NP, NP), f32), pltpu.VMEM((NP,), f32),
@@ -696,14 +693,14 @@
             jax.ShapeDtypeStruct((SIDE, SIDE, NP, EZ), f32),
             jax.ShapeDtypeStruct((1, 1, KC), f32),
         ),
-        in_specs=[vmem] * 5,
+        in_specs=[vmem] * 4,
         out_specs=(hbm, vmem),
         scratch_shapes=[
-            field, pltpu.VMEM((zn, 8, 128), f32), pltpu.VMEM((64, EZ), f32), dma((SIDE,)),
+            field, pltpu.VMEM((64, EZ), f32), dma((SIDE,)),
         ],
         compiler_params=pltpu.CompilerParams(vmem_limit_bytes=20 * 2**20),
         name="finish",
-    )(base, coef, grhs, gpiv, labels)
+    )(base, coef, coarse, labels)
 
 
 def solution(mesh):

time: 33.1 us -> 32.5 us (0.982)
  the two profiles are of different devices: /device:TPU:3 before, /device:TPU:11 now
where the time goes in v6:
time: 32.5 us; the launch traced here: 32.4 us
  Pallas kernels  31.8 us (98%)
  between operations  0.64 us (2%)
    pallas_call x1, Pallas kernels, body(): pl.pallas_call(functools.partial(exchange_kernel, gxn, gyn, zn), out_shap...  29.7 us
    pallas_call x1, Pallas kernels, body(): pl.pallas_call(functools.partial(finish_kernel, gxn, gyn, zn), out_shape=...  2.07 us

profile of v6, /device:TPU:11, one launch (start us, length us, event | category | flops | bytes accessed | tf_op | source)
XLA Modules:
  0.0 32.4 jit_solution(13843750944408482881)
XLA Ops:
  0.6 29.7 %exchange.1 = (f32[16,64,256]{2,1,0:T(8,128)S(1)}, bf16[16,64,256]{2,1,0:T(8,128)(2,1)S(1)}, f32[8,8,128]{2,1,0:T(8,128)S(1)}, f32[32,256]{1,0:T(8,128)S(1)}) custom-call(f32[4,4,64,256]{3,2,1,0:T(8,128)} %rhs_hbm.1, f32[4,4,256]{2,1,0:T(4,128)} %w_hbm.1, s32[4,4,256]{2,1,0:T(4,128)} %agg_hbm.1, f32[64,64]{1,0:T(8,128)} %e_hbm.1, f32[6,64,64]{2,1,0:T(8,128)} %f_hbm.1, ...), custom_call_target="tpu_custom_call" | custom-call | tf_op jit(solution)/shard_map/exchange/pallas_call | solution.py:662
  30.4 2.1 %finish.1 = (f32[4,4,64,256]{3,2,1,0:T(8,128)}, f32[1,1,32]{2,1,0:T(1,128)}) custom-call(f32[16,64,256]{2,1,0:T(8,128)S(1)} %get-tuple-element.6.base_ref, bf16[16,64,256]{2,1,0:T(8,128)(2,1)S(1)} %get-tuple-element.7.coef_ref, f32[8,8,128]{2,1,0:T(8,128)S(1)} %get-tuple-element.8.coarse, f32[32,256]{1,0:T(8,128)S(1)} %get-tuple-element.9.labels), custom_call_target="tpu_custom_call" | custom-call | tf_op jit(solution)/shard_map/finish/pallas_call | solution.py:690
